TPU v7x, 128 devices: a whole 4x4x4 slice. The times are simulated.
128 devices in a mesh: wide: 16 (over x_lo, y, core), narrow: 8 (over x_hi, z).
Axes of the slice: x: 4 (x_hi: 2, x_lo: 2; x = x_hi * 2 + x_lo), y: 4, z: 4, core: 2. Of those that a mesh axis runs over, the one named last changes fastest.
Arguments:
- tokens: bfloat16 [2, 4096, 2048], P(None, 'wide'), may hold values from -6 to 6
- cotangent: bfloat16 [2, 4096, 2048], P(None, 'wide'), may hold values from -6 to 6
- lengths: int32 [2], replicated, may hold values from 256 to 4096, as said below
- query_weight: bfloat16 [2048, 2048], P(None, 'narrow'), may hold values from -0.125 to 0.125
- keyval_weight: bfloat16 [2, 2048, 512], P(None, None, 'narrow'), may hold values from -0.125 to 0.125
- output_weight: bfloat16 [2048, 2048], P('narrow'), may hold values from -0.75 to 0.75
- gateup_weight: bfloat16 [2, 2048, 8192], P(None, None, 'narrow'), may hold values from -1 to 1
- down_weight: bfloat16 [8192, 2048], P('narrow'), may hold values from -0.0625 to 0.0625
- norm_gains: bfloat16 [2, 2048], replicated, may hold values from 0.25 to 3
- query_first: float32 [2048, 2048], P('wide', 'narrow'), may hold values from -9.1552734e-05 to 9.1552734e-05
- keyval_first: float32 [2, 2048, 512], P(None, 'wide', 'narrow'), may hold values from -9.1552734e-05 to 9.1552734e-05
- output_first: float32 [2048, 2048], P('narrow', 'wide'), may hold values from -9.1552734e-05 to 9.1552734e-05
- gateup_first: float32 [2, 2048, 8192], P(None, 'wide', 'narrow'), may hold values from -9.1552734e-05 to 9.1552734e-05
- down_first: float32 [8192, 2048], P('narrow', 'wide'), may hold values from -9.1552734e-05 to 9.1552734e-05
- gains_first: float32 [2, 2048], P(None, 'wide'), may hold values from -9.1552734e-05 to 9.1552734e-05
- query_second: float32 [2048, 2048], P('wide', 'narrow'), may hold values from 4.2748038e-10 to 6.905452e-09
- keyval_second: float32 [2, 2048, 512], P(None, 'wide', 'narrow'), may hold values from 4.2748038e-10 to 6.905452e-09
- output_second: float32 [2048, 2048], P('narrow', 'wide'), may hold values from 5.3435048e-11 to 8.631815e-10
- gateup_second: float32 [2, 2048, 8192], P(None, 'wide', 'narrow'), may hold values from 4.2748038e-10 to 6.905452e-09
- down_second: float32 [8192, 2048], P('narrow', 'wide'), may hold values from 4.2748038e-10 to 6.905452e-09
- gains_second: float32 [2, 2048], P(None, 'wide'), may hold values from 4.2748038e-10 to 6.905452e-09
Outputs:
- layer_out: bfloat16 [2, 4096, 2048], P(None, 'wide')
- input_grad: bfloat16 [2, 4096, 2048], P(None, 'wide')
- query_grad: float32 [2048, 2048], P('wide', 'narrow')
- keyval_grad: float32 [2, 2048, 512], P(None, 'wide', 'narrow')
- output_grad: float32 [2048, 2048], P('narrow', 'wide')
- gateup_grad: float32 [2, 2048, 8192], P(None, 'wide', 'narrow')
- down_grad: float32 [8192, 2048], P('narrow', 'wide')
- gains_grad: float32 [2, 2048], P(None, 'wide')
- grad_norm: float32 [], replicated
- query_momentum: float32 [2048, 2048], P('wide', 'narrow')
- keyval_momentum: float32 [2, 2048, 512], P(None, 'wide', 'narrow')
- output_momentum: float32 [2048, 2048], P('narrow', 'wide')
- gateup_momentum: float32 [2, 2048, 8192], P(None, 'wide', 'narrow')
- down_momentum: float32 [8192, 2048], P('narrow', 'wide')
- gains_momentum: float32 [2, 2048], P(None, 'wide')
- query_variance: float32 [2048, 2048], P('wide', 'narrow')
- keyval_variance: float32 [2, 2048, 512], P(None, 'wide', 'narrow')
- output_variance: float32 [2048, 2048], P('narrow', 'wide')
- gateup_variance: float32 [2, 2048, 8192], P(None, 'wide', 'narrow')
- down_variance: float32 [8192, 2048], P('narrow', 'wide')
- gains_variance: float32 [2, 2048], P(None, 'wide')
- query_updated: float32 [2048, 2048], P('wide', 'narrow')
- keyval_updated: float32 [2, 2048, 512], P(None, 'wide', 'narrow')
- output_updated: float32 [2048, 2048], P('narrow', 'wide')
- gateup_updated: float32 [2, 2048, 8192], P(None, 'wide', 'narrow')
- down_updated: float32 [8192, 2048], P('narrow', 'wide')
- gains_updated: float32 [2, 2048], P(None, 'wide')
Inputs may be any that keep to these rules, and one draw needn't show every extreme that they name: `lengths`: in every draw one bucket, which one drawn from the seed, holds a sequence of all 4096 positions.
All inputs are finite; a program needn't handle non-finite values.
Results may differ from a plain program's by a relative error of at most 0.04.
Values may be sent and summed in bfloat16 or wider, within the bound.
A program may use at most 192 MiB of HBM per device.

v0:
```python
import functools
import math

import jax
import jax.numpy as jnp
import numpy as np
from jax import lax
from jax.experimental import pallas as pl
from jax.experimental.pallas import tpu as pltpu
from jax.sharding import PartitionSpec as P

HD = 64
STEP = 10


norm_eps = 1e-05
rope_theta = 500000.0
rope_factor = 32.0
rope_low = 1.0
rope_high = 4.0
rope_context = 8192.0
clip_limit = 1.0
beta_first = 0.9
beta_second = 0.95
adam_eps = 1e-08
learn_rate = 0.09
gain_rate = 1.2
decay_rate = 0.1
masked_score = -1e30

bf16 = jnp.bfloat16
f32 = jnp.float32
MESH = pl.DeviceIdType.MESH
MB = 1024 * 1024
SLOTS = 7


def lane_tables(positions):
    half_width = HD // 2
    base_freq = rope_theta ** (-np.arange(half_width) * (2.0 / HD))
    wavelen = 2.0 * math.pi / base_freq
    smooth = (rope_context / wavelen - rope_low) / (rope_high - rope_low)
    blended = (1.0 - smooth) * base_freq / rope_factor + smooth * base_freq
    scaled = np.where(
        wavelen < rope_context / rope_high,
        base_freq,
        np.where(wavelen > rope_context / rope_low, base_freq / rope_factor, blended),
    )
    lanes = jnp.asarray(np.tile(scaled, 4), f32)
    sign = jnp.asarray(np.tile(np.repeat([-1.0, 1.0], half_width), 2), f32)
    angles = positions.astype(f32)[:, None] * lanes[None, :]
    return jnp.cos(angles), jnp.sin(angles) * sign[None, :]


def adam_update(weight, gradient, old_first, old_second, step_rate, decay_factor):
    momentum = beta_first * old_first + (1.0 - beta_first) * gradient
    variance = beta_second * old_second + (1.0 - beta_second) * gradient * gradient
    corrected = momentum / (1.0 - beta_first**STEP)
    second_hat = variance / (1.0 - beta_second**STEP)
    updated = weight * (1.0 - step_rate * decay_factor) - step_rate * corrected / (
        jnp.sqrt(second_hat) + adam_eps
    )
    return (updated, momentum, variance)


def dot_nn(a, b):
    return jnp.dot(a, b, preferred_element_type=f32)


def dot_nt(a, b):
    return lax.dot_general(a, b, (((1,), (1,)), ((), ())), preferred_element_type=f32)


def dot_tn(a, b):
    return lax.dot_general(a, b, (((0,), (0,)), ((), ())), preferred_element_type=f32)


def tile(j, size):
    return pl.ds(pl.multiple_of(j * size, size), size)


def greet(targets):
    barrier = pltpu.get_barrier_semaphore()
    for target in targets:
        pl.semaphore_signal(barrier, inc=1, device_id=target, device_id_type=MESH)
    pl.semaphore_wait(barrier, len(targets))


def remote(src, dst, ssem, rsem, there):
    return pltpu.make_async_remote_copy(
        src_ref=src, dst_ref=dst, send_sem=ssem, recv_sem=rsem,
        device_id=there, device_id_type=MESH,
    )


class Grid:
    def __init__(self, axis):
        wide_me, narrow_me = lax.axis_index("wide"), lax.axis_index("narrow")
        self.axis, self.wide_me, self.narrow_me = axis, wide_me, narrow_me
        place = narrow_me if axis == "narrow" else lax.div(wide_me, 2)
        self.core = lax.rem(wide_me, 2)
        self.pair, self.ring = lax.div(place, 4), lax.rem(place, 4)

    def block(self, other, step):
        pair = 1 - self.pair if other else self.pair
        return 4 * pair + lax.rem(self.ring + step + 4, 4)

    def device(self, other, step):
        index = self.block(other, step)
        if self.axis == "narrow":
            return (self.wide_me, index)
        return (2 * index + self.core, self.narrow_me)

    def neighbours(self):
        return [self.device(0, 1), self.device(0, -1), self.device(0, 2), self.device(1, 0)]


def others_of(axis):
    wide_me, narrow_me = lax.axis_index("wide"), lax.axis_index("narrow")
    size = lax.axis_size(axis)
    if axis == "wide":
        return [(lax.rem(wide_me + i, size), narrow_me) for i in range(1, size)]
    return [(wide_me, lax.rem(narrow_me + i, size)) for i in range(1, size)]


def exchange(source, into, axis, ssem, rsem):
    copies = [
        remote(source(there[0]), into.at[i], ssem.at[i], rsem.at[i], there)
        for i, there in enumerate(others_of(axis))
    ]
    for copy in copies:
        copy.start()
    for copy in copies:
        copy.wait()


def mate_of():
    wide_me = lax.axis_index("wide")
    return (wide_me + 1 - 2 * lax.rem(wide_me, 2), lax.axis_index("narrow"))


def mirror_of():
    return (lax.axis_size("wide") - 1 - lax.axis_index("wide"), lax.axis_index("narrow"))


class TreeSum:
    first = (((1, 1), (0, 1)), ((1, -1), (0, -1)), ((1, 2), (1, 0)), ((0, 1), (0, 1)), ((0, -1), (0, -1)))
    second = (((1, 0), (1, 0)), ((0, 2), (0, 2)))

    def __init__(self, grid, part, into, ssem, rsem):
        self.grid, self.part, self.into, self.ssem, self.rsem = grid, part, into, ssem, rsem

    def copy(self, slot):
        block, there = (self.first + self.second)[slot]
        return remote(
            self.part(self.grid.block(*block)), self.into(slot), self.ssem.at[slot],
            self.rsem.at[slot], self.grid.device(*there),
        )

    def start(self):
        for slot in range(5):
            self.copy(slot).start()

    def relay(self, add):
        self.copy(0).wait_recv()
        self.copy(1).wait_recv()
        add(self.grid.block(1, 0), (0, 1))
        self.copy(5).start()
        self.copy(2).wait_recv()
        add(self.grid.block(0, 2), (2,))
        self.copy(6).start()

    def arrive(self):
        for slot in (3, 4, 5, 6):
            self.copy(slot).wait_recv()

    def drain(self):
        for slot in range(SLOTS):
            self.copy(slot).wait_send()


class TreeGather:
    plan = (
        ((0, 0), (1, 0)), ((0, 0), (0, 1)), ((0, 0), (0, -1)), ((0, 0), (0, 2)),
        ((1, 0), (0, 1)), ((1, 0), (0, -1)), ((0, 2), (1, 0)),
    )
    lands = ((1, 0), (0, -1), (0, 1), (0, 2), (1, -1), (1, 1), (1, 2))

    def __init__(self, grid, place, ssem, rsem):
        self.grid, self.place, self.ssem, self.rsem = grid, place, ssem, rsem

    def copy(self, slot):
        block, there = self.plan[slot]
        ref = self.place(self.grid.block(*block))
        return remote(ref, ref, self.ssem.at[slot], self.rsem.at[slot], self.grid.device(*there))

    def start(self):
        for slot in range(4):
            self.copy(slot).start()

    def relay(self):
        self.copy(0).wait_recv()
        self.copy(4).start()
        self.copy(5).start()
        self.copy(3).wait_recv()
        self.copy(6).start()

    def arrive(self):
        for slot in (1, 2, 4, 5, 6):
            self.copy(slot).wait_recv()

    def drain(self):
        for slot in range(SLOTS):
            self.copy(slot).wait_send()


class MateSum:
    def __init__(self, source, own, into, ssem, rsem, lsem=None):
        self.source, self.own, self.into = source, own, into
        self.ssem, self.rsem, self.lsem = ssem, rsem, lsem

    def out(self, k):
        core = lax.rem(lax.axis_index("wide"), 2)
        return remote(
            self.source(2 * k + 1 - core), self.into(k), self.ssem.at[k], self.rsem.at[k], mate_of()
        )

    def start(self):
        def per_block(k, carry):
            self.out(k).start()
            return carry

        lax.fori_loop(0, 8, per_block, 0)

    def add(self):
        core = lax.rem(lax.axis_index("wide"), 2)

        def per_block(k, carry):
            self.out(k).wait_recv()
            self.own(k)[...] = (
                self.source(2 * k + core)[...].astype(f32) + self.into(k)[...].astype(f32)
            ).astype(bf16)
            return carry

        lax.fori_loop(0, 8, per_block, 0)

    def drain(self):
        def per_block(k, carry):
            self.out(k).wait_send()
            return carry

        lax.fori_loop(0, 8, per_block, 0)


def swap_halves(u):
    half = HD // 2
    width = u.shape[-1]
    lane = lax.broadcasted_iota(jnp.int32, u.shape, u.ndim - 1)
    ahead = pltpu.roll(u, width - half, u.ndim - 1)
    behind = pltpu.roll(u, half, u.ndim - 1)
    return jnp.where(lax.rem(lane, HD) < half, ahead, behind)


def inverse_rms(values):
    return lax.rsqrt(jnp.mean(values * values, axis=-1, keepdims=True) + norm_eps)


def head_lanes(pair, odd, high):
    lane = lax.broadcasted_iota(jnp.int32, pair.shape, 1)
    if odd != high:
        pair = pltpu.roll(pair, HD, 1)
    return jnp.where((lane >= HD) == high, pair, 0.0)


def pair_lanes(even, odd):
    lane = lax.broadcasted_iota(jnp.int32, even.shape, 1)
    return jnp.where(lane < HD, even, pltpu.roll(odd, HD, 1))


def block_adder(part, into):
    def add(block, slots):
        total = part(block)[...].astype(f32)
        for slot in slots:
            total = total + into(slot)[...].astype(f32)
        part(block)[...] = total.astype(part(block).dtype)

    return add


class Item:
    def __init__(self, grid, part, into, ssem, rsem, mates=None):
        self.part, self.into, self.mates = part, into, mates
        self.own = grid.block(0, 0)
        self.tree = TreeSum(grid, part, lambda slot: into.at[slot], ssem, rsem)
        self.add = block_adder(part, lambda slot: into.at[slot])

    def relay(self):
        self.tree.relay(self.add)

    def finish(self, out_ref):
        self.tree.arrive()
        height, breadth = out_ref.shape
        span = max(8, min(height, 32768 // breadth))

        def per_tile(j, squares):
            rows = tile(j, span)
            total = self.part(self.own)[rows, :].astype(f32)
            for slot in (3, 4, 5, 6):
                total = total + self.into[slot, rows, :].astype(f32)
            out_ref[rows, :] = total
            return squares + jnp.sum(total * total, axis=0, keepdims=True)

        squares = lax.fori_loop(0, height // span, per_tile, jnp.zeros((1, breadth), f32))
        return jnp.sum(squares, axis=1, keepdims=True)

    def drain(self):
        self.tree.drain()
        if self.mates is not None:
            self.mates.drain()


def key_block(kv, j, bucket, length):
    rows = kv.shape[1] // 2
    block = kv[pl.ds(2 * j, 2), pl.ds(bucket * rows, rows), :].reshape(2 * rows, 2 * HD)
    lane = lax.broadcasted_iota(jnp.int32, block.shape, 1)
    key = 2 * rows * j + lax.broadcasted_iota(jnp.int32, block.shape, 0)
    bias = jnp.where(key < length, 0.0, masked_score)
    masked = jnp.where(lane < HD, block.astype(f32), jnp.where(lane == HD, bias, 0.0)).astype(bf16)
    return block, masked


def head_stack(values, heads, high):
    return jnp.concatenate(
        [
            head_lanes(values[:, (head // 2) * 2 * HD : (head // 2 + 1) * 2 * HD], head % 2 == 1, high)
            for head in range(heads)
        ],
        axis=0,
    )


def forward_kernel(
    len_ref, tok_ref, gains_ref, wq_ref, wkv_ref, cos_ref, sin_ref, wo_hbm, wgu_hbm, wd_hbm, cot_hbm,
    n1_hbm, kv_hbm, qs_ref, os_ref, log_ref, hidden_ref, mixed_ref, dh_ref, gain_ref, dob_ref, gout_ref,
    gate_ref, down_ref, squares_ref, pup_hbm,
    wo, wgu, wd, dyb, n1, kv, q, qm, ob, om, da, n2, dgu, dhb, part1, part2, into1, into2,
    mate_gu, mate_d, gdn, igate, idown,
    in_sem, out_sem, st_sem, kv_s, kv_r, km_s, km_r, ex_s, ex_r, rs_s, rs_r, ag_s, ag_r, mt_s, mt_r, it_s, it_r,
):
    narrow, wide = Grid("narrow"), Grid("wide")
    me, wide_me = narrow.narrow_me, narrow.wide_me
    core = wide.core
    chip = lax.div(wide_me, 2)
    last_chip = lax.axis_size("wide") // 2 - 1
    mate, mirror = mate_of(), mirror_of()
    tokens, width = tok_ref.shape
    rows = tokens // 2
    half = rows // 2
    share = rows // lax.axis_size("narrow")
    units = wd.shape[0]
    heads = wo.shape[0] // HD
    span = 256
    loads = [
        pltpu.make_async_copy(src, dst, in_sem.at[i])
        for i, (src, dst) in enumerate(((wo_hbm, wo), (cot_hbm, dyb), (wd_hbm, wd), (wgu_hbm, wgu)))
    ]
    for load in loads:
        load.start()
    greet(narrow.neighbours() + wide.neighbours() + [mate, mirror])

    def normed(j, carry):
        at = tile(j, 64)
        values = tok_ref[at, :].astype(f32)
        n1[at, :] = (values * inverse_rms(values) * gains_ref[0:1, :].astype(f32)).astype(bf16)
        return carry

    lax.fori_loop(0, tokens // 64, normed, 0)
    cosine = jnp.concatenate([cos_ref[pl.ds(0, rows), :]] * 2, axis=0)
    sine = jnp.concatenate([sin_ref[pl.ds(0, rows), :]] * 2, axis=0)
    value = dot_nt(n1[...], wkv_ref[...])
    lane = lax.broadcasted_iota(jnp.int32, value.shape, 1)
    kv[wide_me] = jnp.where(lane < HD, value * cosine + swap_halves(value) * sine, value).astype(bf16)
    keys = TreeGather(wide, lambda b: kv.at[2 * b + core], kv_s, kv_r)
    keys.start()

    def to_mate(block, i):
        ref = kv.at[2 * block + core]
        return remote(ref, ref, km_s.at[i], km_r.at[i], mate)

    to_mate(chip, 7).start()
    for pair in range(heads // 2):
        columns = pl.ds(pair * 2 * HD, 2 * HD)
        value = dot_nn(n1[...], wq_ref[:, columns])
        q[:, columns] = ((value * cosine + swap_halves(value) * sine) * HD**-0.5).astype(bf16)

    def later(bucket):
        return pl.ds(bucket * rows + half, half)

    queries = [
        remote(q.at[later(b), :], qm.at[b], ex_s.at[0, b], ex_r.at[0, b], mirror) for b in range(2)
    ]
    for copy in queries:
        copy.start()
    store_n1 = pltpu.make_async_copy(n1, n1_hbm, out_sem.at[0])
    store_n1.start()
    keys.relay()
    relayed = [wide.block(1, 0), wide.block(0, 2)]
    for i in range(2):
        to_mate(relayed[i], i).start()
    keys.arrive()
    relayed += [wide.block(*where) for where in ((0, -1), (0, 1), (1, -1), (1, 1), (1, 2))]
    for i in range(2, 7):
        to_mate(relayed[i], i).start()
    for copy in queries:
        copy.wait_recv()
    for b in range(2):
        for g in range(2):
            held = (q[pl.ds(b * rows, half), :] if g == 0 else qm[b]).astype(f32)
            stack = head_stack(held, heads, False)
            lane = lax.broadcasted_iota(jnp.int32, stack.shape, 1)
            qs_ref[b, g] = jnp.where(lane == HD, 1.0, stack).astype(bf16)
    loads[1].wait()
    for b in range(2):
        place = wide_me * rows + lax.broadcasted_iota(jnp.int32, (rows, 1), 0)
        mine = pl.ds(b * rows, rows)
        live = (place < len_ref[b]).astype(f32)
        dyb[mine, :] = (dyb[mine, :].astype(f32) * live).astype(bf16)
    for i in range(7):
        to_mate(relayed[i], i).wait_recv()
    to_mate(chip, 7).wait_recv()
    store_kv = pltpu.make_async_copy(kv, kv_hbm, out_sem.at[1])
    store_kv.start()

    parts = 2
    stack_rows = heads * half
    part_rows = stack_rows // parts

    def attention(b, g):
        length = len_ref[b]
        final = chip if g == 0 else last_chip - chip
        first = wide_me * rows if g == 0 else (2 * last_chip + 1 - wide_me) * rows + half

        def step(masked, j, carry):
            block, scored = key_block(kv, j, b, length)
            lane = lax.broadcasted_iota(jnp.int32, block.shape, 1)
            summed = jnp.where(lane < HD, jnp.ones_like(block), block)
            if masked:
                shape = (part_rows, 2 * rows)
                key = 2 * rows * j + lax.broadcasted_iota(jnp.int32, shape, 1)
                place = first + lax.rem(lax.broadcasted_iota(jnp.int32, shape, 0), half)
                allowed = key <= place
            result = []
            for p in range(parts):
                best, total = carry[p]
                scores = dot_nt(qs_ref[b, g, pl.ds(p * part_rows, part_rows), :], scored)
                if masked:
                    scores = jnp.where(allowed, scores, masked_score)
                new_best = jnp.maximum(best, jnp.max(scores, axis=-1, keepdims=True))
                weights = jnp.exp(scores - new_best).astype(bf16)
                total = total * jnp.exp(best - new_best) + dot_nn(weights, summed)
                result.append((new_best, total))
            return tuple(result)

        carry = tuple(
            (jnp.full((part_rows, 1), masked_score, f32), jnp.zeros((part_rows, 2 * HD), f32))
            for _ in range(parts)
        )
        carry = lax.fori_loop(0, final, functools.partial(step, False), carry)
        carry = step(True, final, carry)
        for p in range(parts):
            best, total = carry[p]
            lane = lax.broadcasted_iota(jnp.int32, total.shape, 1)
            sums = jnp.where(lane < HD, total, pltpu.roll(total, HD, 1))
            out = total / sums
            at = pl.ds(p * part_rows, part_rows)
            os_ref[b, g, at, :] = out
            logs = jnp.transpose(best + jnp.log(sums))
            log_ref[pl.ds(2 * b + g, 1), at] = logs[0:1, :]
        for pair in range(heads // 2):
            even = os_ref[b, g, pl.ds(2 * pair * half, half), :]
            odd = os_ref[b, g, pl.ds((2 * pair + 1) * half, half), :]
            value = pair_lanes(pltpu.roll(even, HD, 1), pltpu.roll(odd, HD, 1)).astype(bf16)
            columns = pl.ds(pair * 2 * HD, 2 * HD)
            if g == 0:
                ob[pl.ds(b * rows, half), columns] = value
            else:
                om[b, :, columns] = value

    def back_to_mirror(b):
        return remote(om.at[b], ob.at[later(b), :], ex_s.at[1, b], ex_r.at[1, b], mirror)

    def mine_in(b):
        return pl.ds(pl.multiple_of(b * rows + me * share, share), share)

    def their_rows(b):
        return lambda block: pl.ds(pl.multiple_of(b * rows + block * share, share), share)

    def sum_of(b, part, into, number):
        where = their_rows(b)
        return TreeSum(
            narrow, lambda block: part.at[where(block), :], lambda slot: into.at[b, slot],
            rs_s.at[number, b], rs_r.at[number, b],
        )

    def adder(b, part, into):
        where = their_rows(b)

        def add(block, slots):
            total = part[where(block), :].astype(f32)
            for slot in slots:
                total = total + into[b, slot].astype(f32)
            part[where(block), :] = total.astype(bf16)

        return add

    def total_of(b, part, into):
        total = part[mine_in(b), :].astype(f32)
        for slot in (3, 4, 5, 6):
            total = total + into[b, slot].astype(f32)
        return total

    def gather_of(b, buffer, number):
        where = their_rows(b)
        return TreeGather(
            narrow, lambda block: buffer.at[where(block), :], ag_s.at[number, b], ag_r.at[number, b]
        )

    sums1 = [sum_of(b, part1, into1, 0) for b in range(2)]
    sums2 = [sum_of(b, part2, into2, 1) for b in range(2)]
    gather1 = [gather_of(b, n2, 0) for b in range(2)]
    gather2 = [gather_of(b, dhb, 1) for b in range(2)]

    def project(b):
        back_to_mirror(b).wait_recv()
        mine = pl.ds(b * rows, rows)
        part1[mine, :] = dot_nn(ob[mine, :], wo[...]).astype(bf16)
        sums1[b].start()

    attention(0, 1)
    back_to_mirror(0).start()
    attention(0, 0)
    loads[0].wait()
    project(0)
    attention(1, 1)
    back_to_mirror(1).start()
    attention(1, 0)
    project(1)
    sums1[0].relay(adder(0, part1, into1))
    loads[2].wait()

    def grad_middle(j, carry):
        da[:, tile(j, span)] = dot_nt(dyb[...], wd[tile(j, span), :])
        return carry

    lax.fori_loop(0, units // span, grad_middle, 0)
    sums1[1].relay(adder(1, part1, into1))
    gain2 = gains_ref[1:2, :].astype(f32)
    gain_ref[...] = jnp.zeros(gain_ref.shape, f32)

    def second_norm(b):
        sums1[b].arrive()
        hidden = tok_ref[mine_in(b), :].astype(f32) + total_of(b, part1, into1)
        hidden_ref[b] = hidden
        n2[mine_in(b), :] = (hidden * inverse_rms(hidden) * gain2).astype(bf16)
        gather1[b].start()

    second_norm(0)
    second_norm(1)
    loads[3].wait()
    gather1[0].relay()
    gather1[1].relay()

    def feed(b):
        gather1[b].arrive()
        mine = pl.ds(b * rows, rows)

        def gate_up(j, carry):
            columns = tile(j, span)
            gate = dot_nn(n2[mine, :], wgu[0, :, columns])
            up = dot_nn(n2[mine, :], wgu[1, :, columns])
            sigmoid = jax.nn.sigmoid(gate)
            activated = gate * sigmoid
            mixed_ref[mine, columns] = (activated * up).astype(bf16)
            grad = da[mine, columns]
            dgu[0, mine, columns] = (
                grad * up * sigmoid * (1.0 + gate * (1.0 - sigmoid))
            ).astype(bf16)
            dgu[1, mine, columns] = (grad * activated).astype(bf16)
            return carry

        lax.fori_loop(0, units // span, gate_up, 0)

        def grad_norm_two(c, carry):
            columns = tile(c, 512)
            part2[mine, columns] = (
                dot_nt(dgu[0, mine, :], wgu[0, columns, :]) + dot_nt(dgu[1, mine, :], wgu[1, columns, :])
            ).astype(bf16)
            return carry

        lax.fori_loop(0, width // 512, grad_norm_two, 0)
        sums2[b].start()

    feed(0)
    feed(1)
    wide_share = width // 16
    mates = [
        MateSum(
            lambda w, i=i: wgu.at[i, tile(w, wide_share), :],
            lambda k, i=i: wgu.at[i, tile(2 * k + core, wide_share), :],
            lambda k, i=i: mate_gu.at[i, k], mt_s.at[i], mt_r.at[i],
        )
        for i in range(2)
    ]
    mates.append(
        MateSum(
            lambda w: gdn.at[w], lambda k: gdn.at[2 * k + core], lambda k: mate_d.at[k],
            mt_s.at[2], mt_r.at[2],
        )
    )
    gate = Item(wide, mates[0].own, igate, it_s.at[0], it_r.at[0], mates[0])
    down = Item(wide, mates[2].own, idown, it_s.at[1], it_r.at[1], mates[2])

    def grad_down(j, carry):
        found = dot_tn(mixed_ref[:, tile(j, span)], dyb[...]).astype(bf16)
        for w in range(16):
            gdn[w, tile(j, span), :] = found[:, w * wide_share : (w + 1) * wide_share]
        return carry

    def grad_gateup(which):
        def per_tile(j, carry):
            wgu[which, tile(j, span), :] = dot_tn(n2[:, tile(j, span)], dgu[which]).astype(bf16)
            return carry

        lax.fori_loop(0, width // span, per_tile, 0)

    def second_norm_back(b):
        sums2[b].arrive()
        total = total_of(b, part2, into2)
        hidden = hidden_ref[b]
        inverse = inverse_rms(hidden)
        z2 = hidden * inverse
        gain_ref[pl.ds(b, 1), :] = jnp.sum(total * z2, axis=0, keepdims=True)
        weighted = total * gain2
        dh = dyb[mine_in(b), :].astype(f32) + inverse * (
            weighted - z2 * jnp.mean(weighted * z2, axis=-1, keepdims=True)
        )
        dh_ref[b] = dh
        dhb[mine_in(b), :] = dh.astype(bf16)
        gather2[b].start()

    lax.fori_loop(0, units // span, grad_down, 0)
    mates[2].start()
    sums2[0].relay(adder(0, part2, into2))
    grad_gateup(0)
    mates[0].start()
    sums2[1].relay(adder(1, part2, into2))
    second_norm_back(0)
    mates[2].add()
    down.tree.start()
    second_norm_back(1)
    mates[0].add()
    gate.tree.start()
    gather2[0].relay()
    grad_gateup(1)
    mates[1].start()
    gather2[1].relay()
    down.relay()
    for b in range(2):
        gather2[b].arrive()
        mine = pl.ds(b * rows, rows)
        dob_ref[mine, :] = dot_nt(dhb[mine, :], wo[...]).astype(bf16)

    def grad_out(j, carry):
        gout_ref[:, tile(j, span)] = dot_tn(ob[...], dhb[:, tile(j, span)]).astype(bf16)
        return carry

    lax.fori_loop(0, width // span, grad_out, 0)
    gate.relay()
    mates[1].add()

    def kept(k):
        return pltpu.make_async_copy(mates[1].own(k), pup_hbm.at[k], st_sem.at[k])

    def keep(k, carry):
        kept(k).start()
        return carry

    lax.fori_loop(0, 8, keep, 0)
    squares = down.finish(down_ref) + gate.finish(gate_ref)
    squares_ref[...] = jnp.broadcast_to(squares, squares_ref.shape)
    for b in range(2):
        sums1[b].drain()
        sums2[b].drain()
        gather1[b].drain()
        gather2[b].drain()
        queries[b].wait_send()
        back_to_mirror(b).wait_send()
    keys.drain()
    for i in range(7):
        to_mate(relayed[i], i).wait_send()
    to_mate(chip, 7).wait_send()
    gate.drain()
    down.drain()
    mates[1].drain()
    store_n1.wait()
    store_kv.wait()

    def per_store(k, carry):
        kept(k).wait()
        return carry

    lax.fori_loop(0, 8, per_store, 0)


def forward(lengths, tokens, gains, wq, wkv, cosine, sine, wo, wgu, wd, cotangent):
    count, width = tokens.shape
    rows = count // 2
    share = rows // 8
    units = wd.shape[0]
    lanes = wq.shape[1]
    heads = lanes // HD
    stack = heads * rows // 2
    wide_count = 16
    wide_share = width // wide_count
    here = pl.BlockSpec(memory_space=pltpu.VMEM)
    anywhere = pl.BlockSpec(memory_space=pl.ANY)
    shape = jax.ShapeDtypeStruct
    dma = pltpu.SemaphoreType.DMA
    vmem = pltpu.VMEM
    return pl.pallas_call(
        forward_kernel,
        out_shape=(
            shape((count, width), bf16),
            shape((wide_count, count, 2 * HD), bf16),
            shape((2, 2, stack, 2 * HD), bf16),
            shape((2, 2, stack, 2 * HD), f32),
            shape((8, stack), f32),
            shape((2, share, width), f32),
            shape((count, units), bf16),
            shape((2, share, width), f32),
            shape((8, width), f32),
            shape((count, lanes), bf16),
            shape((lanes, width), bf16),
            shape((wide_share, units), f32),
            shape((units, wide_share), f32),
            shape((8, wide_share), f32),
            shape((8, wide_share, units), bf16),
        ),
        in_specs=[pl.BlockSpec(memory_space=pltpu.SMEM)] + [here] * 6 + [anywhere] * 4,
        out_specs=(anywhere, anywhere) + (here,) * 12 + (anywhere,),
        scratch_shapes=[
            vmem(wo.shape, bf16),
            vmem(wgu.shape, bf16),
            vmem(wd.shape, bf16),
            vmem((count, width), bf16),
            vmem((count, width), bf16),
            vmem((wide_count, count, 2 * HD), bf16),
            vmem((count, lanes), bf16),
            vmem((2, rows // 2, lanes), bf16),
            vmem((count, lanes), bf16),
            vmem((2, rows // 2, lanes), bf16),
            vmem((count, units), f32),
            vmem((count, width), bf16),
            vmem((2, count, units), bf16),
            vmem((count, width), bf16),
            vmem((count, width), bf16),
            vmem((count, width), bf16),
            vmem((2, SLOTS, share, width), bf16),
            vmem((2, SLOTS, share, width), bf16),
            vmem((2, 8, wide_share, units), bf16),
            vmem((8, units, wide_share), bf16),
            vmem((wide_count, units, wide_share), bf16),
            vmem((SLOTS, wide_share, units), bf16),
            vmem((SLOTS, units, wide_share), bf16),
            dma((4,)),
            dma((2,)),
            dma((8,)),
            dma((SLOTS,)),
            dma((SLOTS,)),
            dma((8,)),
            dma((8,)),
            dma((2, 2)),
            dma((2, 2)),
            dma((2, 2, SLOTS)),
            dma((2, 2, SLOTS)),
            dma((2, 2, SLOTS)),
            dma((2, 2, SLOTS)),
            dma((3, 8)),
            dma((3, 8)),
            dma((2, SLOTS)),
            dma((2, SLOTS)),
        ],
        compiler_params=pltpu.CompilerParams(
            collective_id=1, has_side_effects=True, vmem_limit_bytes=63 * MB
        ),
        name="forward",
    )(lengths, tokens, gains, wq, wkv, cosine, sine, wo, wgu, wd, cotangent)


def backward_kernel(
    len_ref, tok_hbm, gains_ref, wq_ref, wkv_ref, cos_ref, sin_ref,
    qs_ref, os_ref, log_ref, hidden_ref, mixed_ref, dh_ref, gain2_ref, dob_ref, gout_ref,
    squares_ref, kv_hbm, n1_hbm, wd_hbm, pup_hbm,
    layer_ref, grad_ref, q_ref, pair_ref, out_ref, up_ref, gains_out_ref, norm_ref,
    kv, n1, wd, tok, pup, pout, pq, pkv, iup, iout, iq, ikv,
    mout, mq, mkv, gq, gkv, part3, part4, into3, into4, acc, dkv, dkm, dkin, dkv_low, dq, dqm, dm,
    dos, qclean, delta, dqacc, gpart, gin, near_own, near, norm_own, norm_in, pair,
    ld_sem, rs_s, rs_r, ag_s, ag_r, dm_s, dm_r, dt_s, dt_r, im_s, im_r, it_s, it_r, ex_s, ex_r,
    g_s, g_r, h_s, h_r, w_s, w_r,
):
    narrow, wide = Grid("narrow"), Grid("wide")
    me, wide_me = narrow.narrow_me, narrow.wide_me
    core = wide.core
    chip = lax.div(wide_me, 2)
    last_chip = lax.axis_size("wide") // 2 - 1
    peers = lax.axis_size("narrow")
    mate, mirror = mate_of(), mirror_of()
    tokens, width = layer_ref.shape
    rows = tokens // 2
    half = rows // 2
    share = rows // peers
    heads = wq_ref.shape[1] // HD
    span = 256
    wide_share = width // 16

    def mine_in(b):
        return pl.ds(pl.multiple_of(b * rows + me * share, share), share)

    def later(b):
        return pl.ds(b * rows + half, half)

    moves = (
        (kv_hbm, kv), (wd_hbm, wd), (pup_hbm, pup), (n1_hbm, n1),
        (tok_hbm.at[mine_in(0), :], tok.at[0]), (tok_hbm.at[mine_in(1), :], tok.at[1]),
    )
    loads = [pltpu.make_async_copy(src, dst, ld_sem.at[i]) for i, (src, dst) in enumerate(moves)]
    for load in loads:
        load.start()
    greet(others_of("narrow") + others_of("wide"))

    grads_there = [
        remote(dob_ref.at[later(b), :], dm.at[b], ex_s.at[0, b], ex_r.at[0, b], mirror) for b in range(2)
    ]
    for copy in grads_there:
        copy.start()

    def mates_of(source, own, into, number):
        return MateSum(
            source, lambda k: own.at[k], lambda k: into.at[k], im_s.at[number], im_r.at[number]
        )

    up = Item(wide, lambda b: pup.at[b], iup, it_s.at[0], it_r.at[0])
    out = Item(
        wide, lambda b: pout.at[b], iout, it_s.at[1], it_r.at[1],
        mates_of(lambda w: gout_ref.at[:, tile(w, wide_share)], pout, mout, 0),
    )
    query = Item(
        wide, lambda b: pq.at[b], iq, it_s.at[2], it_r.at[2],
        mates_of(lambda w: gq.at[tile(w, wide_share), :], pq, mq, 1),
    )
    keyval = Item(
        wide, lambda b: pkv.at[b], ikv, it_s.at[3], it_r.at[3],
        mates_of(lambda w: gkv.at[tile(w, wide_share), :], pkv, mkv, 2),
    )
    out.mates.start()

    def their_rows(b):
        return lambda block: pl.ds(pl.multiple_of(b * rows + block * share, share), share)

    def sum_of(b, part, into, number):
        where = their_rows(b)
        return TreeSum(
            narrow, lambda block: part.at[where(block), :], lambda slot: into.at[b, slot],
            rs_s.at[number, b], rs_r.at[number, b],
        )

    def adder(b, part, into):
        where = their_rows(b)
        return block_adder(lambda block: part.at[where(block), :], lambda slot: into.at[b, slot])

    def total_of(b, part, into):
        total = part[mine_in(b), :].astype(f32)
        for slot in (3, 4, 5, 6):
            total = total + into[b, slot].astype(f32)
        return total

    def gather_of(b, buffer, number):
        where = their_rows(b)
        return TreeGather(
            narrow, lambda block: buffer.at[where(block), :], ag_s.at[number, b], ag_r.at[number, b]
        )

    sums3 = [sum_of(b, part3, into3, 0) for b in range(2)]
    sums4 = [sum_of(b, part4, into4, 1) for b in range(2)]
    gather3 = [gather_of(b, layer_ref, 0) for b in range(2)]
    gather4 = [gather_of(b, grad_ref, 1) for b in range(2)]

    loads[1].wait()
    for b in range(2):
        mine = pl.ds(b * rows, rows)

        def feed(c, carry):
            part3[mine, tile(c, 512)] = dot_nn(mixed_ref[mine, :], wd[:, tile(c, 512)]).astype(bf16)
            return carry

        lax.fori_loop(0, width // 512, feed, 0)
        sums3[b].start()
    loads[2].wait()
    up.tree.start()
    loads[0].wait()
    stack_rows = heads * half
    parts = 2
    part_rows = stack_rows // parts

    def attention(b, g):
        length = len_ref[b]
        final = chip if g == 0 else last_chip - chip
        first = wide_me * rows if g == 0 else (2 * last_chip + 1 - wide_me) * rows + half
        held = (dob_ref[pl.ds(b * rows, half), :] if g == 0 else dm[b]).astype(f32)
        stack = head_stack(held, heads, True)
        dos[...] = stack.astype(bf16)
        for p in range(parts):
            at = pl.ds(p * part_rows, part_rows)
            product = stack[p * part_rows : (p + 1) * part_rows] * os_ref[b, g, at, :]
            delta[:, at] = jnp.sum(jnp.transpose(product), axis=0, keepdims=True)
        lane = lax.broadcasted_iota(jnp.int32, qclean.shape, 1)
        qclean[...] = jnp.where(lane < HD, qs_ref[b, g].astype(f32), 0.0).astype(bf16)
        dqacc[...] = jnp.zeros(dqacc.shape, f32)

        def step(masked, j, carry):
            block, scored = key_block(kv, j, b, length)
            if masked:
                shape = (2 * rows, part_rows)
                key = 2 * rows * j + lax.broadcasted_iota(jnp.int32, shape, 0)
                place = first + lax.rem(lax.broadcasted_iota(jnp.int32, shape, 1), half)
                allowed = key <= place
            total = acc[j]
            for p in range(parts):
                at = pl.ds(p * part_rows, part_rows)
                scores = dot_nt(scored, qs_ref[b, g, at, :])
                if masked:
                    scores = jnp.where(allowed, scores, masked_score)
                chances = jnp.exp(scores - log_ref[pl.ds(2 * b + g, 1), at])
                slope = (chances * (dot_nt(block, dos[at, :]) - delta[:, at])).astype(bf16)
                total = total + dot_nn(slope, qclean[at, :]) + dot_nn(chances.astype(bf16), dos[at, :])
                dqacc[at, :] = dqacc[at, :] + dot_tn(slope, block)
            acc[j] = total
            return carry

        lax.fori_loop(0, final, functools.partial(step, False), 0)
        step(True, final, 0)
        for pair in range(heads // 2):
            even = dqacc[pl.ds(2 * pair * half, half), :]
            odd = dqacc[pl.ds((2 * pair + 1) * half, half), :]
            value = pair_lanes(even, odd) * HD**-0.5
            table = pl.ds(0, half) if g == 0 else pl.ds(rows, half)
            value = (value * cos_ref[table, :] - swap_halves(value) * sin_ref[table, :]).astype(bf16)
            columns = pl.ds(pair * 2 * HD, 2 * HD)
            if g == 0:
                dq[pl.ds(b * rows, half), columns] = value
            else:
                dqm[b, :, columns] = value

    def query_back(b):
        return remote(dqm.at[b], dq.at[later(b), :], ex_s.at[1, b], ex_r.at[1, b], mirror)

    def clear():
        def per_block(j, carry):
            acc[j] = jnp.zeros(acc.shape[1:], f32)
            return carry

        lax.fori_loop(0, acc.shape[0], per_block, 0)

    pair_mates = [
        MateSum(
            lambda w, b=b: dkv.at[b, w], lambda k, b=b: dkv.at[b, 2 * k + core],
            lambda k, b=b: dkm.at[b, k], dm_s.at[b], dm_r.at[b],
        )
        for b in range(2)
    ]
    pair_trees = [
        TreeSum(
            wide, lambda block, b=b: dkv.at[b, 2 * block + core], lambda slot, b=b: dkin.at[b, slot],
            dt_s.at[b], dt_r.at[b],
        )
        for b in range(2)
    ]

    def pair_relay(b):
        pair_trees[b].relay(
            block_adder(lambda block: dkv.at[b, 2 * block + core], lambda slot: dkin.at[b, slot])
        )

    def pair_send(b):
        def per_block(j, carry):
            dkv[b, pl.ds(2 * j, 2)] = acc[j].astype(bf16).reshape(2, rows, 2 * HD)
            return carry

        lax.fori_loop(0, acc.shape[0], per_block, 0)
        pair_mates[b].start()

    def pair_mid(b):
        pair_mates[b].add()
        pair_trees[b].start()

    def pair_total(b):
        pair_trees[b].arrive()
        total = dkv[b, wide_me].astype(f32)
        for slot in (3, 4, 5, 6):
            total = total + dkin[b, slot].astype(f32)
        mine = pl.ds(b * rows, rows)
        lane = lax.broadcasted_iota(jnp.int32, total.shape, 1)
        table = pl.ds(0, rows)
        turned = total * cos_ref[table, :] - swap_halves(total) * sin_ref[table, :]
        dkv_low[mine, :] = jnp.where(lane < HD, turned, total).astype(bf16)

    def norm_one_back(b):
        mine = pl.ds(b * rows, rows)

        def per_chunk(c, carry):
            columns = tile(c, 512)
            part4[mine, columns] = (
                dot_nt(dq[mine, :], wq_ref[columns, :]) + dot_nn(dkv_low[mine, :], wkv_ref[:, columns])
            ).astype(bf16)
            return carry

        lax.fori_loop(0, width // 512, per_chunk, 0)
        sums4[b].start()

    def result_rows(b):
        sums3[b].arrive()
        layer_ref[mine_in(b), :] = (hidden_ref[b] + total_of(b, part3, into3)).astype(bf16)
        gather3[b].start()

    gains1 = gains_ref[0:1, :].astype(f32)

    def input_rows(b):
        sums4[b].arrive()
        total = total_of(b, part4, into4)
        values = tok[b].astype(f32)
        inverse = inverse_rms(values)
        z1 = values * inverse
        weighted = total * gains1
        grad_ref[mine_in(b), :] = (
            dh_ref[b] + inverse * (weighted - z1 * jnp.mean(weighted * z1, axis=-1, keepdims=True))
        ).astype(bf16)
        gather4[b].start()
        return jnp.sum(total * z1, axis=0, keepdims=True)

    clear()
    for copy in grads_there:
        copy.wait_recv()
    attention(0, 1)
    query_back(0).start()
    attention(0, 0)
    pair_send(0)
    sums3[0].relay(adder(0, part3, into3))
    sums3[1].relay(adder(1, part3, into3))
    clear()
    attention(1, 1)
    query_back(1).start()
    pair_mid(0)
    result_rows(0)
    result_rows(1)
    attention(1, 0)
    pair_send(1)
    pair_relay(0)
    pair_mid(1)
    pair_total(0)
    query_back(0).wait_recv()
    norm_one_back(0)
    gather3[0].relay()
    gather3[1].relay()
    query_back(1).wait_recv()
    loads[3].wait()

    def grad_query(j, carry):
        gq[tile(j, span), :] = dot_tn(n1[:, tile(j, span)], dq[...]).astype(bf16)
        return carry

    pair_relay(1)
    lax.fori_loop(0, width // span, grad_query, 0)
    query.mates.start()
    sums4[0].relay(adder(0, part4, into4))
    pair_total(1)
    norm_one_back(1)

    def grad_keyval(j, carry):
        gkv[tile(j, span), :] = dot_tn(n1[:, tile(j, span)], dkv_low[...]).astype(bf16)
        return carry

    query.mates.add()
    query.tree.start()
    out.mates.add()
    out.tree.start()
    lax.fori_loop(0, width // span, grad_keyval, 0)
    keyval.mates.start()
    up.relay()
    loads[4].wait()
    loads[5].wait()
    gain1 = input_rows(0)
    keyval.mates.add()
    keyval.tree.start()
    sums4[1].relay(adder(1, part4, into4))
    query.relay()
    out.relay()
    gather4[0].relay()
    keyval.relay()
    squares = squares_ref[0:1, 0:1] + up.finish(up_ref)
    gain1 = gain1 + input_rows(1)

    row = lax.broadcasted_iota(jnp.int32, gpart.shape, 0)
    gain2 = gain2_ref[0:1, :] + gain2_ref[1:2, :]
    gpart[...] = jnp.where(row == 0, gain1, jnp.where(row == 1, gain2, 0.0))
    gain_copies = [
        remote(gpart.at[:, tile(there[0], wide_share)], gin.at[i], g_s.at[i], g_r.at[i], there)
        for i, there in enumerate(others_of("wide"))
    ]
    for copy in gain_copies:
        copy.start()
    squares = squares + query.finish(q_ref) + out.finish(out_ref)
    share_kv = keyval.finish(pair)
    pair_ref[...] = jnp.transpose(pair[...])
    squares = squares + share_kv
    gather4[1].relay()
    for copy in gain_copies:
        copy.wait()
    total = gpart[:, tile(wide_me, wide_share)]
    for i in range(len(gain_copies)):
        total = total + gin[i]
    row = lax.broadcasted_iota(jnp.int32, total.shape, 0)
    near_own[...] = jnp.where(row < 2, total, jnp.broadcast_to(squares, total.shape))
    exchange(lambda index: near_own, near, "narrow", h_s, h_r)
    total = near_own[...]
    for i in range(peers - 1):
        total = total + near[i]
    gains_out_ref[...] = total
    kept = jnp.where(row < 2, total, 0.0)
    gain_squares = jnp.sum(jnp.sum(kept * kept, axis=1, keepdims=True), axis=0, keepdims=True)
    norm_own[...] = total[2:3, :] + jnp.broadcast_to(gain_squares, norm_own.shape)
    exchange(lambda index: norm_own, norm_in, "wide", w_s, w_r)
    total = norm_own[...]
    for i in range(len(gain_copies)):
        total = total + norm_in[i]
    norm_ref[...] = jnp.sqrt(total)
    for b in range(2):
        gather3[b].arrive()
        gather4[b].arrive()
        for each in (sums3[b], sums4[b], gather3[b], gather4[b], pair_mates[b], pair_trees[b]):
            each.drain()
        grads_there[b].wait_send()
        query_back(b).wait_send()
    for item in (up, out, query, keyval):
        item.drain()


def backward(
    lengths, tokens, gains, wq, wkv, cosine, sine, qs, outs, logs, hidden, mixed, dh, gain2,
    dob, gout, squares, kv, n1, wd, pup,
):
    count, width = n1.shape
    rows = count // 2
    share = rows // 8
    units = wd.shape[0]
    lanes = wq.shape[1]
    stack = qs.shape[2]
    wide_count = 16
    wide_share = width // wide_count
    here = pl.BlockSpec(memory_space=pltpu.VMEM)
    anywhere = pl.BlockSpec(memory_space=pl.ANY)
    shape = jax.ShapeDtypeStruct
    dma = pltpu.SemaphoreType.DMA
    vmem = pltpu.VMEM
    blocks = (
        (wide_share, units), (lanes, wide_share),
        (wide_share, lanes), (wide_share, 2 * HD),
    )
    return pl.pallas_call(
        backward_kernel,
        out_shape=(
            shape((count, width), bf16),
            shape((count, width), bf16),
            shape((wide_share, lanes), f32),
            shape((2 * HD, wide_share), f32),
            shape((lanes, wide_share), f32),
            shape((wide_share, units), f32),
            shape((8, wide_share), f32),
            shape((8, wide_share), f32),
        ),
        in_specs=[pl.BlockSpec(memory_space=pltpu.SMEM), anywhere] + [here] * 15 + [anywhere] * 4,
        out_specs=(here,) * 8,
        scratch_shapes=[
            vmem(kv.shape, bf16),
            vmem((count, width), bf16),
            vmem(wd.shape, bf16),
            vmem((2, share, width), bf16),
            *[vmem((8, *block), bf16) for block in blocks],
            *[vmem((SLOTS, *block), bf16) for block in blocks],
            *[vmem((8, *block), bf16) for block in blocks[1:]],
            vmem((width, lanes), bf16),
            vmem((width, 2 * HD), bf16),
            vmem((count, width), bf16),
            vmem((count, width), bf16),
            vmem((2, SLOTS, share, width), bf16),
            vmem((2, SLOTS, share, width), bf16),
            vmem((8, 2 * rows, 2 * HD), f32),
            vmem((2, wide_count, rows, 2 * HD), bf16),
            vmem((2, 8, rows, 2 * HD), bf16),
            vmem((2, SLOTS, rows, 2 * HD), bf16),
            vmem((count, 2 * HD), bf16),
            vmem((count, lanes), bf16),
            vmem((2, rows // 2, lanes), bf16),
            vmem((2, rows // 2, lanes), bf16),
            vmem((stack, 2 * HD), bf16),
            vmem((stack, 2 * HD), bf16),
            vmem((1, stack), f32),
            vmem((stack, 2 * HD), f32),
            vmem((8, width), f32),
            vmem((wide_count - 1, 8, wide_share), f32),
            vmem((8, wide_share), f32),
            vmem((7, 8, wide_share), f32),
            vmem((8, wide_share), f32),
            vmem((wide_count - 1, 8, wide_share), f32),
            vmem((wide_share, 2 * HD), f32),
            dma((6,)),
            dma((2, 2, SLOTS)),
            dma((2, 2, SLOTS)),
            dma((2, 2, SLOTS)),
            dma((2, 2, SLOTS)),
            dma((2, 8)),
            dma((2, 8)),
            dma((2, SLOTS)),
            dma((2, SLOTS)),
            dma((3, 8)),
            dma((3, 8)),
            dma((4, SLOTS)),
            dma((4, SLOTS)),
            dma((2, 2)),
            dma((2, 2)),
            dma((wide_count - 1,)),
            dma((wide_count - 1,)),
            dma((7,)),
            dma((7,)),
            dma((wide_count - 1,)),
            dma((wide_count - 1,)),
        ],
        compiler_params=pltpu.CompilerParams(
            collective_id=2, has_side_effects=True, vmem_limit_bytes=63 * MB
        ),
        name="backward",
    )(
        lengths, tokens, gains, wq, wkv, cosine, sine, qs, outs, logs, hidden, mixed, dh,
        gain2, dob, gout, squares, kv, n1, wd, pup,
    )


def update_kernel(
    norm_ref, gains_sum_ref, gains_ref, gains_first_ref, gains_second_ref, *refs
):
    count = 6
    grads, weights, firsts, seconds = (refs[i * count : (i + 1) * count] for i in range(4))
    refs = refs[4 * count :]
    (layer, grad), refs = refs[:2], refs[2:]
    outs, refs = [refs[i * count : (i + 1) * count] for i in range(4)], refs[4 * count :]
    (layer_out, grad_out), refs = refs[:2], refs[2:]
    gain_outs, refs = refs[:4], refs[4:]
    held, refs = [refs[i * count : (i + 1) * count] for i in range(5)], refs[5 * count :]
    rows_held, in_sem, out_sem, copy_sem = refs
    wide_me = lax.axis_index("wide")
    at = tile(wide_me, 128)
    slices = (
        lambda ref: ref.at[:, at], lambda ref: ref.at[0, at, :], lambda ref: ref.at[1, at, :],
        lambda ref: ref.at[:, at], lambda ref: ref.at[at, :], lambda ref: ref.at[:, at],
    )
    halves = (None, 0, 1, None, None, None)
    loads, stores = [], []
    for i in range(count):
        def whole(ref):
            return ref if halves[i] is None else ref.at[halves[i]]

        sources = (grads[i], slices[i](weights[i]), whole(firsts[i]), whole(seconds[i]))
        loads.append(
            [pltpu.make_async_copy(src, held[n][i], in_sem.at[n, i]) for n, src in enumerate(sources)]
        )
        targets = (
            (held[0][i], outs[0][i]), (held[2][i], outs[1][i]), (held[3][i], outs[2][i]),
            (held[4][i], outs[3][i]),
        )
        stores.append(
            [
                pltpu.make_async_copy(src, whole(dst), out_sem.at[n, i])
                for n, (src, dst) in enumerate(targets)
            ]
        )
    for group in loads:
        for load in group:
            load.start()
    moved_in = [
        pltpu.make_async_copy(src, rows_held.at[n], copy_sem.at[n]) for n, src in enumerate((layer, grad))
    ]
    moved_out = [
        pltpu.make_async_copy(rows_held.at[n], dst, copy_sem.at[2 + n])
        for n, dst in enumerate((layer_out, grad_out))
    ]
    for copy in moved_in:
        copy.start()
    factor = jnp.minimum(1.0, clip_limit / (norm_ref[0:1, 0:1] + 1e-06))

    for i in range(count):
        for load in loads[i]:
            load.wait()
        height, breadth = held[0][i].shape
        span = max(8, min(height, 16384 // breadth))

        def step(j, carry):
            rows = tile(j, span)
            clipped = held[0][i][rows, :] * factor
            updated, momentum, variance = adam_update(
                held[1][i][rows, :].astype(f32), clipped, held[2][i][rows, :], held[3][i][rows, :],
                learn_rate, decay_rate,
            )
            held[0][i][rows, :] = clipped
            held[2][i][rows, :] = momentum
            held[3][i][rows, :] = variance
            held[4][i][rows, :] = updated
            return carry

        lax.fori_loop(0, height // span, step, 0)
        for store in stores[i]:
            store.start()
    for before, after in zip(moved_in, moved_out):
        before.wait()
        after.start()
    clipped = gains_sum_ref[0:2, :] * factor
    updated, momentum, variance = adam_update(
        gains_ref[:, at].astype(f32), clipped, gains_first_ref[...], gains_second_ref[...], gain_rate, 0.0
    )
    for ref, value in zip(gain_outs, (clipped, momentum, variance, updated)):
        ref[...] = value
    for group in stores:
        for store in group:
            store.wait()
    for copy in moved_out:
        copy.wait()


def update(norm, gains_sum, gains, gains_first, gains_second, grads, weights, firsts, seconds, layer, grad):
    here = pl.BlockSpec(memory_space=pltpu.VMEM)
    anywhere = pl.BlockSpec(memory_space=pl.ANY)
    shape = jax.ShapeDtypeStruct
    like = [shape(first.shape, f32) for first in firsts]
    kept = [like[0], like[1], like[3], like[4], like[5]]
    blocks = [grad_part.shape for grad_part in grads]
    small = shape(gains_first.shape, f32)
    dma = pltpu.SemaphoreType.DMA

    def body(*refs):
        head, rest = refs[:5], refs[5:]
        ins, rest = rest[:6], rest[6:]
        groups = []
        for _ in range(3):
            down, gateup, out, query, keyval = rest[:5]
            groups += [down, gateup, gateup, out, query, keyval]
            rest = rest[5:]
        moved, rest = rest[:2], rest[2:]
        outs = []
        for _ in range(4):
            down, gateup, out, query, keyval = rest[:5]
            outs += [down, gateup, gateup, out, query, keyval]
            rest = rest[5:]
        update_kernel(*head, *ins, *groups, *moved, *outs, *rest)

    def five(arrays):
        return [arrays[0], arrays[1], arrays[3], arrays[4], arrays[5]]

    return pl.pallas_call(
        body,
        out_shape=tuple(kept * 4 + [shape(layer.shape, bf16), shape(grad.shape, bf16)] + [small] * 4),
        in_specs=[here] * 5 + [anywhere] * 23,
        out_specs=tuple([anywhere] * 22 + [here] * 4),
        scratch_shapes=[
            *[pltpu.VMEM(block, f32) for block in blocks],
            *[pltpu.VMEM(block, bf16) for block in blocks],
            *[pltpu.VMEM(block, f32) for block in blocks * 3],
            pltpu.VMEM((2, *layer.shape), bf16),
            dma((4, 6)),
            dma((4, 6)),
            dma((4,)),
        ],
        compiler_params=pltpu.CompilerParams(vmem_limit_bytes=63 * MB),
        name="update",
    )(
        norm, gains_sum, gains, gains_first, gains_second, *grads, *five(weights), *five(firsts),
        *five(seconds), layer, grad,
    )


def shards(
    tokens,
    cotangent,
    lengths,
    query_weight,
    keyval_weight,
    output_weight,
    gateup_weight,
    down_weight,
    norm_gains,
    query_first,
    keyval_first,
    output_first,
    gateup_first,
    down_first,
    gains_first,
    query_second,
    keyval_second,
    output_second,
    gateup_second,
    down_second,
    gains_second,
):
    bucket_count, row_count, model_width = tokens.shape
    wide_count = lax.axis_size("wide")
    wide_rank = lax.axis_index("wide")
    token_count = bucket_count * row_count
    half = row_count // 2
    mirror_rank = wide_count - 1 - wide_rank
    positions = jnp.concatenate(
        [
            wide_rank * row_count + jnp.arange(row_count, dtype=jnp.int32),
            mirror_rank * row_count + half + jnp.arange(half, dtype=jnp.int32),
        ]
    )
    cosine, sine = lane_tables(positions)
    inputs = tokens.reshape(token_count, model_width)
    units = down_weight.shape[0]

    def turned(values):
        return values.transpose(0, 2, 1).reshape(2 * HD, -1)

    def turned_back(values):
        return values.reshape(2, HD, -1).transpose(0, 2, 1)

    pair_weight = turned(keyval_weight)
    (
        normed_one, pairs, query_stack, out_stack, logs, hidden, mixed, grad_hidden, gain_two, grad_heads,
        output_grad, gate_sum, down_sum, squares, up_part,
    ) = forward(
        lengths, inputs, norm_gains, query_weight, pair_weight, cosine, sine, output_weight,
        gateup_weight, down_weight, cotangent.reshape(token_count, model_width),
    )
    layer_rows, grad_rows, query_sum, pair_sum, output_sum, up_sum, gains_sum, norm = backward(
        lengths, inputs, norm_gains, query_weight, pair_weight, cosine, sine, query_stack, out_stack,
        logs, hidden, mixed, grad_hidden, gain_two, grad_heads, output_grad, squares, pairs, normed_one,
        down_weight, up_part,
    )
    results = update(
        norm, gains_sum, norm_gains, gains_first, gains_second,
        (down_sum, gate_sum, up_sum, output_sum, query_sum, pair_sum),
        (down_weight, gateup_weight, gateup_weight, output_weight, query_weight, pair_weight),
        (down_first, gateup_first, gateup_first, output_first, query_first, turned(keyval_first)),
        (down_second, gateup_second, gateup_second, output_second, query_second, turned(keyval_second)),
        layer_rows, grad_rows,
    )
    layer_out = results[20].reshape(bucket_count, row_count, model_width)
    input_grad = results[21].reshape(bucket_count, row_count, model_width)
    kinds = []
    for kind in range(4):
        down, gateup, output, query, pair = results[5 * kind : 5 * kind + 5]
        kinds.append((query, turned_back(pair), output, gateup, down, results[22 + kind]))
    clipped, momentum, variance, updated = kinds
    return (
        layer_out, input_grad, *clipped, norm[0, 0], *momentum, *variance, *updated,
    )


def solution(mesh):
    return jax.shard_map(
        shards,
        mesh=mesh,
        in_specs=(
            P(None, "wide", None),
            P(None, "wide", None),
            P(),
            P(None, "narrow"),
            P(None, None, "narrow"),
            P("narrow", None),
            P(None, None, "narrow"),
            P("narrow", None),
            P(),
            P("wide", "narrow"),
            P(None, "wide", "narrow"),
            P("narrow", "wide"),
            P(None, "wide", "narrow"),
            P("narrow", "wide"),
            P(None, "wide"),
            P("wide", "narrow"),
            P(None, "wide", "narrow"),
            P("narrow", "wide"),
            P(None, "wide", "narrow"),
            P("narrow", "wide"),
            P(None, "wide"),
        ),
        out_specs=(
            P(None, "wide", None),
            P(None, "wide", None),
            P("wide", "narrow"),
            P(None, "wide", "narrow"),
            P("narrow", "wide"),
            P(None, "wide", "narrow"),
            P("narrow", "wide"),
            P(None, "wide"),
            P(),
            P("wide", "narrow"),
            P(None, "wide", "narrow"),
            P("narrow", "wide"),
            P(None, "wide", "narrow"),
            P("narrow", "wide"),
            P(None, "wide"),
            P("wide", "narrow"),
            P(None, "wide", "narrow"),
            P("narrow", "wide"),
            P(None, "wide", "narrow"),
            P("narrow", "wide"),
            P(None, "wide"),
            P("wide", "narrow"),
            P(None, "wide", "narrow"),
            P("narrow", "wide"),
            P(None, "wide", "narrow"),
            P("narrow", "wide"),
            P(None, "wide"),
        ),
        check_vma=False,
    )
```

profile of v0, /device:TPU:1, one launch (start us, length us, event | category | flops | bytes accessed | tf_op | source)
XLA Modules:
  0.0 256.8 jit_solution(4438256005920739113)
XLA Ops:
  0.7 2.2 fusion
  2.9 138.4 %forward.1 = (bf16[512,2048]{1,0:T(8,128)(2,1)}, bf16[16,512,128]{2,1,0:T(8,128)(2,1)}, bf16[2,2,512,128]{3,2,1,0:T(8,128)(2,1)}, f32[2,2,512,128]{3,2,1,0:T(8,1...) custom-call(s32[2]{0:T(128)} %len_ref.3, ...), custom_call_target="tpu_custom_call" | custom-call | tf_op jit(solution)/shard_map/forward/pallas_call | solution.py:730
  141.4 104.4 %backward.1 = (bf16[512,2048]{1,0:T(8,128)(2,1)}, bf16[512,2048]{1,0:T(8,128)(2,1)}, f32[128,256]{1,0:T(8,128)}, f32[128,128]{1,0:T(8,128)}, f32[256,128]{1,0:T(...) custom-call(s32[2]{0:T(128)} %len_ref.3, bf16[512,2048]{1,0:T(8,128)(2,1)} %bitcast.27, ...), custom_call_target="tpu_custom_call" | custom-call | tf_op jit(solution)/shard_map/backward/pallas_call | solution.py:1178
  245.8 9.9 %update.1 = (f32[1024,128]{1,0:T(8,128)}, f32[2,128,1024]{2,1,0:T(8,128)}, f32[256,128]{1,0:T(8,128)}, f32[128,256]{1,0:T(8,128)}, f32[128,128]{1,0:T(8,128)}, /...) custom-call(f32[8,128]{1,0:T(8,128)} %get-tuple-element.89.refs_0_, ...), custom_call_target="tpu_custom_call" | custom-call | tf_op jit(solution)/shard_map/update/pallas_call | solution.py:1376
  255.7 1.2 slice.3
  (3 shorter events, 0.0 us)
where the time goes:
time: 257 us
  Pallas kernels  253 us (98%)
    pallas_call x1, Pallas kernels, forward(): pl.pallas_call(forward_kernel, out_shape=(shape((count, width), bf16), sh...  138 us
    pallas_call x1, Pallas kernels, backward(): pl.pallas_call(backward_kernel, out_shape=(shape((count, width), bf16), s...  104 us
    pallas_call x1, Pallas kernels, update(): pl.pallas_call(body, out_shape=tuple(kept * 4 + [shape(layer.shape, bf16)...  9.91 us

commit v1 on v0

--- a/solution.py
+++ b/solution.py
@@ -35,7 +35,7 @@
 SLOTS = 7
 
 
-def lane_tables(positions):
+def rotation_tables(wide_count, row_count):
     half_width = HD // 2
     base_freq = rope_theta ** (-np.arange(half_width) * (2.0 / HD))
     wavelen = 2.0 * math.pi / base_freq
@@ -46,10 +46,12 @@
         base_freq,
         np.where(wavelen > rope_context / rope_low, base_freq / rope_factor, blended),
     )
-    lanes = jnp.asarray(np.tile(scaled, 4), f32)
-    sign = jnp.asarray(np.tile(np.repeat([-1.0, 1.0], half_width), 2), f32)
-    angles = positions.astype(f32)[:, None] * lanes[None, :]
-    return jnp.cos(angles), jnp.sin(angles) * sign[None, :]
+    lanes = np.tile(scaled, 4)[None, :]
+    inside = np.arange(row_count)[:, None] * lanes
+    starts = np.arange(wide_count)[:, None] * row_count * lanes
+    sign = np.tile(np.repeat([-1.0, 1.0], half_width), 2)[None, :]
+    tables = (np.cos(inside), np.sin(inside), np.cos(starts), np.sin(starts), sign)
+    return tuple(jnp.asarray(table, f32) for table in tables)
 
 
 def adam_update(weight, gradient, old_first, old_second, step_rate, decay_factor):
@@ -83,7 +85,18 @@
     barrier = pltpu.get_barrier_semaphore()
     for target in targets:
         pl.semaphore_signal(barrier, inc=1, device_id=target, device_id_type=MESH)
-    pl.semaphore_wait(barrier, len(targets))
+
+
+def met(targets):
+    pl.semaphore_wait(pltpu.get_barrier_semaphore(), len(targets))
+
+
+def rotation(tables, rank, first, count):
+    cos_in, sin_in, cos_rank, sin_rank, sign = tables
+    rows = pl.ds(first, count)
+    c_in, s_in = cos_in[rows, :], sin_in[rows, :]
+    c_rank, s_rank = cos_rank[pl.ds(rank, 1), :], sin_rank[pl.ds(rank, 1), :]
+    return c_in * c_rank - s_in * s_rank, (s_in * c_rank + c_in * s_rank) * sign[...]
 
 
 def remote(src, dst, ssem, rsem, there):
@@ -340,11 +353,13 @@
 
 
 def forward_kernel(
-    len_ref, tok_ref, gains_ref, wq_ref, wkv_ref, cos_ref, sin_ref, wo_hbm, wgu_hbm, wd_hbm, cot_hbm,
-    n1_hbm, kv_hbm, qs_ref, os_ref, log_ref, hidden_ref, mixed_ref, dh_ref, gain_ref, dob_ref, gout_ref,
-    gate_ref, down_ref, squares_ref, pup_hbm,
+    len_ref, tok_ref, gains_ref, wkv_ref, tab0, tab1, tab2, tab3, tab4, wq_hbm, wo_hbm, wgu_hbm, wd_hbm,
+    cot_hbm,
+    log_ref, dh_ref, gain_ref, dob_ref, gout_ref, down_ref, squares_ref,
+    n1_hbm, kv_hbm, qs_hbm, os_hbm, hidden_hbm, mixed_hbm, pgate_hbm, pup_hbm,
+    wq_ref, qs_ref, os_ref, hidden_ref, mixed_ref,
     wo, wgu, wd, dyb, n1, kv, q, qm, ob, om, da, n2, dgu, dhb, part1, part2, into1, into2,
-    mate_gu, mate_d, gdn, igate, idown,
+    mate_gu, mate_d, gdn, idown,
     in_sem, out_sem, st_sem, kv_s, kv_r, km_s, km_r, ex_s, ex_r, rs_s, rs_r, ag_s, ag_r, mt_s, mt_r, it_s, it_r,
 ):
     narrow, wide = Grid("narrow"), Grid("wide")
@@ -362,11 +377,14 @@
     span = 256
     loads = [
         pltpu.make_async_copy(src, dst, in_sem.at[i])
-        for i, (src, dst) in enumerate(((wo_hbm, wo), (cot_hbm, dyb), (wd_hbm, wd), (wgu_hbm, wgu)))
+        for i, (src, dst) in enumerate(
+            ((wo_hbm, wo), (cot_hbm, dyb), (wd_hbm, wd), (wgu_hbm, wgu), (wq_hbm, wq_ref))
+        )
     ]
-    for load in loads:
-        load.start()
-    greet(narrow.neighbours() + wide.neighbours() + [mate, mirror])
+    partners = narrow.neighbours() + wide.neighbours() + [mate, mirror]
+    greet(partners)
+    for i in (4, 1, 0, 2, 3):
+        loads[i].start()
 
     def normed(j, carry):
         at = tile(j, 64)
@@ -375,19 +393,27 @@
         return carry
 
     lax.fori_loop(0, tokens // 64, normed, 0)
-    cosine = jnp.concatenate([cos_ref[pl.ds(0, rows), :]] * 2, axis=0)
-    sine = jnp.concatenate([sin_ref[pl.ds(0, rows), :]] * 2, axis=0)
+    cosine, sine = rotation((tab0, tab1, tab2, tab3, tab4), wide_me, 0, rows)
+    cosine, sine = jnp.concatenate([cosine] * 2, axis=0), jnp.concatenate([sine] * 2, axis=0)
     value = dot_nt(n1[...], wkv_ref[...])
     lane = lax.broadcasted_iota(jnp.int32, value.shape, 1)
     kv[wide_me] = jnp.where(lane < HD, value * cosine + swap_halves(value) * sine, value).astype(bf16)
-    keys = TreeGather(wide, lambda b: kv.at[2 * b + core], kv_s, kv_r)
-    keys.start()
-
-    def to_mate(block, i):
-        ref = kv.at[2 * block + core]
-        return remote(ref, ref, km_s.at[i], km_r.at[i], mate)
-
-    to_mate(chip, 7).start()
+    met(partners)
+
+    def keys_at(b):
+        bucket = pl.ds(b * rows, rows)
+        return lambda block: kv.at[2 * block + core, bucket, :]
+
+    keys = [TreeGather(wide, keys_at(b), kv_s.at[b], kv_r.at[b]) for b in range(2)]
+
+    def to_mate(b, block, i):
+        ref = keys_at(b)(block)
+        return remote(ref, ref, km_s.at[b, i], km_r.at[b, i], mate)
+
+    for b in range(2):
+        keys[b].start()
+        to_mate(b, chip, 7).start()
+    loads[4].wait()
     for pair in range(heads // 2):
         columns = pl.ds(pair * 2 * HD, 2 * HD)
         value = dot_nn(n1[...], wq_ref[:, columns])
@@ -401,39 +427,52 @@
     ]
     for copy in queries:
         copy.start()
-    store_n1 = pltpu.make_async_copy(n1, n1_hbm, out_sem.at[0])
-    store_n1.start()
-    keys.relay()
-    relayed = [wide.block(1, 0), wide.block(0, 2)]
-    for i in range(2):
-        to_mate(relayed[i], i).start()
-    keys.arrive()
-    relayed += [wide.block(*where) for where in ((0, -1), (0, 1), (1, -1), (1, 1), (1, 2))]
-    for i in range(2, 7):
-        to_mate(relayed[i], i).start()
-    for copy in queries:
-        copy.wait_recv()
+
+    def store(src, dst, i):
+        return pltpu.make_async_copy(src, dst, out_sem.at[i])
+
+    store(n1, n1_hbm, 0).start()
+    relayed = [
+        wide.block(*where) for where in ((1, 0), (0, 2), (0, -1), (0, 1), (1, -1), (1, 1), (1, 2))
+    ]
+
+    def keys_relay(b):
+        keys[b].relay()
+        for i in range(2):
+            to_mate(b, relayed[i], i).start()
+
+    def keys_arrive(b):
+        keys[b].arrive()
+        for i in range(2, 7):
+            to_mate(b, relayed[i], i).start()
+
+    def keys_complete(b):
+        for i in range(7):
+            to_mate(b, relayed[i], i).wait_recv()
+        to_mate(b, chip, 7).wait_recv()
+
+    def stack_queries(b, g):
+        held = (q[pl.ds(b * rows, half), :] if g == 0 else qm[b]).astype(f32)
+        stack = head_stack(held, heads, False)
+        lane = lax.broadcasted_iota(jnp.int32, stack.shape, 1)
+        qs_ref[b, g] = jnp.where(lane == HD, 1.0, stack).astype(bf16)
+
     for b in range(2):
-        for g in range(2):
-            held = (q[pl.ds(b * rows, half), :] if g == 0 else qm[b]).astype(f32)
-            stack = head_stack(held, heads, False)
-            lane = lax.broadcasted_iota(jnp.int32, stack.shape, 1)
-            qs_ref[b, g] = jnp.where(lane == HD, 1.0, stack).astype(bf16)
+        stack_queries(b, 0)
+    keys_relay(0)
     loads[1].wait()
     for b in range(2):
         place = wide_me * rows + lax.broadcasted_iota(jnp.int32, (rows, 1), 0)
         mine = pl.ds(b * rows, rows)
         live = (place < len_ref[b]).astype(f32)
         dyb[mine, :] = (dyb[mine, :].astype(f32) * live).astype(bf16)
-    for i in range(7):
-        to_mate(relayed[i], i).wait_recv()
-    to_mate(chip, 7).wait_recv()
-    store_kv = pltpu.make_async_copy(kv, kv_hbm, out_sem.at[1])
-    store_kv.start()
-
-    parts = 2
+    keys_relay(1)
+    for b in range(2):
+        queries[b].wait_recv()
+        stack_queries(b, 1)
+    keys_arrive(0)
+
     stack_rows = heads * half
-    part_rows = stack_rows // parts
 
     def attention(b, g):
         length = len_ref[b]
@@ -444,38 +483,24 @@
             block, scored = key_block(kv, j, b, length)
             lane = lax.broadcasted_iota(jnp.int32, block.shape, 1)
             summed = jnp.where(lane < HD, jnp.ones_like(block), block)
+            scores = dot_nt(qs_ref[b, g], scored)
             if masked:
-                shape = (part_rows, 2 * rows)
-                key = 2 * rows * j + lax.broadcasted_iota(jnp.int32, shape, 1)
-                place = first + lax.rem(lax.broadcasted_iota(jnp.int32, shape, 0), half)
-                allowed = key <= place
-            result = []
-            for p in range(parts):
-                best, total = carry[p]
-                scores = dot_nt(qs_ref[b, g, pl.ds(p * part_rows, part_rows), :], scored)
-                if masked:
-                    scores = jnp.where(allowed, scores, masked_score)
-                new_best = jnp.maximum(best, jnp.max(scores, axis=-1, keepdims=True))
-                weights = jnp.exp(scores - new_best).astype(bf16)
-                total = total * jnp.exp(best - new_best) + dot_nn(weights, summed)
-                result.append((new_best, total))
-            return tuple(result)
-
-        carry = tuple(
-            (jnp.full((part_rows, 1), masked_score, f32), jnp.zeros((part_rows, 2 * HD), f32))
-            for _ in range(parts)
-        )
+                key = 2 * rows * j + lax.broadcasted_iota(jnp.int32, scores.shape, 1)
+                place = first + lax.rem(lax.broadcasted_iota(jnp.int32, scores.shape, 0), half)
+                scores = jnp.where(key <= place, scores, masked_score)
+            best, total = carry
+            new_best = jnp.maximum(best, jnp.max(scores, axis=-1, keepdims=True))
+            weights = jnp.exp(scores - new_best).astype(bf16)
+            return new_best, total * jnp.exp(best - new_best) + dot_nn(weights, summed)
+
+        carry = (jnp.full((stack_rows, 1), masked_score, f32), jnp.zeros((stack_rows, 2 * HD), f32))
         carry = lax.fori_loop(0, final, functools.partial(step, False), carry)
-        carry = step(True, final, carry)
-        for p in range(parts):
-            best, total = carry[p]
-            lane = lax.broadcasted_iota(jnp.int32, total.shape, 1)
-            sums = jnp.where(lane < HD, total, pltpu.roll(total, HD, 1))
-            out = total / sums
-            at = pl.ds(p * part_rows, part_rows)
-            os_ref[b, g, at, :] = out
-            logs = jnp.transpose(best + jnp.log(sums))
-            log_ref[pl.ds(2 * b + g, 1), at] = logs[0:1, :]
+        best, total = step(True, final, carry)
+        lane = lax.broadcasted_iota(jnp.int32, total.shape, 1)
+        sums = jnp.where(lane < HD, total, pltpu.roll(total, HD, 1))
+        os_ref[b, g] = total / sums
+        logs = jnp.transpose(best + jnp.log(sums))
+        log_ref[pl.ds(2 * b + g, 1), :] = logs[0:1, :]
         for pair in range(heads // 2):
             even = os_ref[b, g, pl.ds(2 * pair * half, half), :]
             odd = os_ref[b, g, pl.ds((2 * pair + 1) * half, half), :]
@@ -536,14 +561,20 @@
         part1[mine, :] = dot_nn(ob[mine, :], wo[...]).astype(bf16)
         sums1[b].start()
 
+    keys_complete(0)
     attention(0, 1)
     back_to_mirror(0).start()
+    keys_arrive(1)
     attention(0, 0)
     loads[0].wait()
     project(0)
+    keys_complete(1)
+    store(kv, kv_hbm, 1).start()
     attention(1, 1)
     back_to_mirror(1).start()
     attention(1, 0)
+    store(os_ref, os_hbm, 2).start()
+    store(qs_ref, qs_hbm, 3).start()
     project(1)
     sums1[0].relay(adder(0, part1, into1))
     loads[2].wait()
@@ -602,6 +633,8 @@
 
     feed(0)
     feed(1)
+    store(hidden_ref, hidden_hbm, 4).start()
+    store(mixed_ref, mixed_hbm, 5).start()
     wide_share = width // 16
     mates = [
         MateSum(
@@ -617,8 +650,7 @@
             mt_s.at[2], mt_r.at[2],
         )
     )
-    gate = Item(wide, mates[0].own, igate, it_s.at[0], it_r.at[0], mates[0])
-    down = Item(wide, mates[2].own, idown, it_s.at[1], it_r.at[1], mates[2])
+    down = Item(wide, mates[2].own, idown, it_s, it_r, mates[2])
 
     def grad_down(j, carry):
         found = dot_tn(mixed_ref[:, tile(j, span)], dyb[...]).astype(bf16)
@@ -648,23 +680,34 @@
         dhb[mine_in(b), :] = dh.astype(bf16)
         gather2[b].start()
 
+    def kept(which, out_hbm, k):
+        return pltpu.make_async_copy(mates[which].own(k), out_hbm.at[k], st_sem.at[which, k])
+
+    def keep(which, out_hbm):
+        mates[which].add()
+
+        def per_block(k, carry):
+            kept(which, out_hbm, k).start()
+            return carry
+
+        lax.fori_loop(0, 8, per_block, 0)
+
     lax.fori_loop(0, units // span, grad_down, 0)
     mates[2].start()
     sums2[0].relay(adder(0, part2, into2))
     grad_gateup(0)
+    mates[2].add()
+    down.tree.start()
     mates[0].start()
     sums2[1].relay(adder(1, part2, into2))
     second_norm_back(0)
-    mates[2].add()
-    down.tree.start()
     second_norm_back(1)
-    mates[0].add()
-    gate.tree.start()
     gather2[0].relay()
     grad_gateup(1)
     mates[1].start()
     gather2[1].relay()
     down.relay()
+    keep(0, pgate_hbm)
     for b in range(2):
         gather2[b].arrive()
         mine = pl.ds(b * rows, rows)
@@ -675,19 +718,8 @@
         return carry
 
     lax.fori_loop(0, width // span, grad_out, 0)
-    gate.relay()
-    mates[1].add()
-
-    def kept(k):
-        return pltpu.make_async_copy(mates[1].own(k), pup_hbm.at[k], st_sem.at[k])
-
-    def keep(k, carry):
-        kept(k).start()
-        return carry
-
-    lax.fori_loop(0, 8, keep, 0)
-    squares = down.finish(down_ref) + gate.finish(gate_ref)
-    squares_ref[...] = jnp.broadcast_to(squares, squares_ref.shape)
+    keep(1, pup_hbm)
+    squares_ref[...] = jnp.broadcast_to(down.finish(down_ref), squares_ref.shape)
     for b in range(2):
         sums1[b].drain()
         sums2[b].drain()
@@ -695,24 +727,27 @@
         gather2[b].drain()
         queries[b].wait_send()
         back_to_mirror(b).wait_send()
-    keys.drain()
-    for i in range(7):
-        to_mate(relayed[i], i).wait_send()
-    to_mate(chip, 7).wait_send()
-    gate.drain()
+        keys[b].drain()
+        for i in range(7):
+            to_mate(b, relayed[i], i).wait_send()
+        to_mate(b, chip, 7).wait_send()
     down.drain()
+    mates[0].drain()
     mates[1].drain()
-    store_n1.wait()
-    store_kv.wait()
-
-    def per_store(k, carry):
-        kept(k).wait()
-        return carry
-
-    lax.fori_loop(0, 8, per_store, 0)
-
-
-def forward(lengths, tokens, gains, wq, wkv, cosine, sine, wo, wgu, wd, cotangent):
+    for i, (src, dst) in enumerate(
+        ((n1, n1_hbm), (kv, kv_hbm), (os_ref, os_hbm), (qs_ref, qs_hbm), (hidden_ref, hidden_hbm),
+         (mixed_ref, mixed_hbm))
+    ):
+        store(src, dst, i).wait()
+    for which, out_hbm in ((0, pgate_hbm), (1, pup_hbm)):
+        def per_store(k, carry):
+            kept(which, out_hbm, k).wait()
+            return carry
+
+        lax.fori_loop(0, 8, per_store, 0)
+
+
+def forward(lengths, tokens, gains, wkv, tables, wq, wo, wgu, wd, cotangent):
     count, width = tokens.shape
     rows = count // 2
     share = rows // 8
@@ -730,25 +765,30 @@
     return pl.pallas_call(
         forward_kernel,
         out_shape=(
+            shape((8, stack), f32),
+            shape((2, share, width), f32),
+            shape((8, width), f32),
+            shape((count, lanes), bf16),
+            shape((lanes, width), bf16),
+            shape((units, wide_share), f32),
+            shape((8, wide_share), f32),
             shape((count, width), bf16),
             shape((wide_count, count, 2 * HD), bf16),
             shape((2, 2, stack, 2 * HD), bf16),
             shape((2, 2, stack, 2 * HD), f32),
-            shape((8, stack), f32),
             shape((2, share, width), f32),
             shape((count, units), bf16),
-            shape((2, share, width), f32),
-            shape((8, width), f32),
-            shape((count, lanes), bf16),
-            shape((lanes, width), bf16),
-            shape((wide_share, units), f32),
-            shape((units, wide_share), f32),
-            shape((8, wide_share), f32),
+            shape((8, wide_share, units), bf16),
             shape((8, wide_share, units), bf16),
         ),
-        in_specs=[pl.BlockSpec(memory_space=pltpu.SMEM)] + [here] * 6 + [anywhere] * 4,
-        out_specs=(anywhere, anywhere) + (here,) * 12 + (anywhere,),
+        in_specs=[pl.BlockSpec(memory_space=pltpu.SMEM)] + [here] * 8 + [anywhere] * 5,
+        out_specs=(here,) * 7 + (anywhere,) * 8,
         scratch_shapes=[
+            vmem(wq.shape, bf16),
+            vmem((2, 2, stack, 2 * HD), bf16),
+            vmem((2, 2, stack, 2 * HD), f32),
+            vmem((2, share, width), f32),
+            vmem((count, units), bf16),
             vmem(wo.shape, bf16),
             vmem(wgu.shape, bf16),
             vmem(wd.shape, bf16),
@@ -770,15 +810,14 @@
             vmem((2, 8, wide_share, units), bf16),
             vmem((8, units, wide_share), bf16),
             vmem((wide_count, units, wide_share), bf16),
-            vmem((SLOTS, wide_share, units), bf16),
             vmem((SLOTS, units, wide_share), bf16),
-            dma((4,)),
-            dma((2,)),
-            dma((8,)),
-            dma((SLOTS,)),
-            dma((SLOTS,)),
-            dma((8,)),
-            dma((8,)),
+            dma((5,)),
+            dma((6,)),
+            dma((2, 8)),
+            dma((2, SLOTS)),
+            dma((2, SLOTS)),
+            dma((2, 8)),
+            dma((2, 8)),
             dma((2, 2)),
             dma((2, 2)),
             dma((2, 2, SLOTS)),
@@ -787,26 +826,27 @@
             dma((2, 2, SLOTS)),
             dma((3, 8)),
             dma((3, 8)),
-            dma((2, SLOTS)),
-            dma((2, SLOTS)),
+            dma((SLOTS,)),
+            dma((SLOTS,)),
         ],
         compiler_params=pltpu.CompilerParams(
             collective_id=1, has_side_effects=True, vmem_limit_bytes=63 * MB
         ),
         name="forward",
-    )(lengths, tokens, gains, wq, wkv, cosine, sine, wo, wgu, wd, cotangent)
+    )(lengths, tokens, gains, wkv, *tables, wq, wo, wgu, wd, cotangent)
 
 
 def backward_kernel(
-    len_ref, tok_hbm, gains_ref, wq_ref, wkv_ref, cos_ref, sin_ref,
-    qs_ref, os_ref, log_ref, hidden_ref, mixed_ref, dh_ref, gain2_ref, dob_ref, gout_ref,
-    squares_ref, kv_hbm, n1_hbm, wd_hbm, pup_hbm,
-    layer_ref, grad_ref, q_ref, pair_ref, out_ref, up_ref, gains_out_ref, norm_ref,
+    len_ref, gains_ref, tab0, tab1, tab2, tab3, tab4, log_ref, mixed_ref, gain2_ref, dob_ref, squares_ref,
+    qs_ref, os_ref, tok_hbm, wq_hbm, wkv_hbm, hidden_hbm, dh_hbm, gout_hbm, kv_hbm, n1_hbm, wd_hbm,
+    pgate_hbm, pup_hbm,
+    q_ref, pair_ref, out_ref, gate_ref, up_ref, gains_out_ref, norm_ref, layer_hbm, grad_hbm,
+    layer_ref, grad_ref, wq_ref, wkv_ref, hidden_ref, dh_ref, gout_ref, cos_ref, sin_ref, pgate, igate,
     kv, n1, wd, tok, pup, pout, pq, pkv, iup, iout, iq, ikv,
     mout, mq, mkv, gq, gkv, part3, part4, into3, into4, acc, dkv, dkm, dkin, dkv_low, dq, dqm, dm,
-    dos, qclean, delta, dqacc, gpart, gin, near_own, near, norm_own, norm_in, pair,
-    ld_sem, rs_s, rs_r, ag_s, ag_r, dm_s, dm_r, dt_s, dt_r, im_s, im_r, it_s, it_r, ex_s, ex_r,
-    g_s, g_r, h_s, h_r, w_s, w_r,
+    dos, qclean, delta, dqacc, grow, gpart, gnear, gwide, spart, snear, pair,
+    ld_sem, out_sem, rs_s, rs_r, ag_s, ag_r, dm_s, dm_r, dt_s, dt_r, im_s, im_r, it_s, it_r, ex_s, ex_r,
+    g_s, g_r, h_s, h_r,
 ):
     narrow, wide = Grid("narrow"), Grid("wide")
     me, wide_me = narrow.narrow_me, narrow.wide_me
@@ -832,11 +872,27 @@
     moves = (
         (kv_hbm, kv), (wd_hbm, wd), (pup_hbm, pup), (n1_hbm, n1),
         (tok_hbm.at[mine_in(0), :], tok.at[0]), (tok_hbm.at[mine_in(1), :], tok.at[1]),
+        (pgate_hbm, pgate), (gout_hbm, gout_ref), (hidden_hbm, hidden_ref), (wq_hbm, wq_ref),
+        (wkv_hbm, wkv_ref), (dh_hbm, dh_ref),
     )
     loads = [pltpu.make_async_copy(src, dst, ld_sem.at[i]) for i, (src, dst) in enumerate(moves)]
-    for load in loads:
-        load.start()
-    greet(others_of("narrow") + others_of("wide"))
+    partners = others_of("narrow") + others_of("wide")
+    greet(partners)
+    for i in (1, 0, 2, 6, 7, 8, 9, 10, 3, 4, 5, 11):
+        loads[i].start()
+    tables = (tab0, tab1, tab2, tab3, tab4)
+    cos_ref[pl.ds(0, rows), :], sin_ref[pl.ds(0, rows), :] = rotation(tables, wide_me, 0, rows)
+    cos_ref[pl.ds(rows, half), :], sin_ref[pl.ds(rows, half), :] = rotation(
+        tables, 2 * last_chip + 1 - wide_me, half, half
+    )
+    loads[1].wait()
+
+    def feed(c, carry):
+        part3[:, tile(c, 512)] = dot_nn(mixed_ref[...], wd[:, tile(c, 512)]).astype(bf16)
+        return carry
+
+    lax.fori_loop(0, width // 512, feed, 0)
+    met(partners)
 
     grads_there = [
         remote(dob_ref.at[later(b), :], dm.at[b], ex_s.at[0, b], ex_r.at[0, b], mirror) for b in range(2)
@@ -850,6 +906,7 @@
         )
 
     up = Item(wide, lambda b: pup.at[b], iup, it_s.at[0], it_r.at[0])
+    gate = Item(wide, lambda b: pgate.at[b], igate, it_s.at[4], it_r.at[4])
     out = Item(
         wide, lambda b: pout.at[b], iout, it_s.at[1], it_r.at[1],
         mates_of(lambda w: gout_ref.at[:, tile(w, wide_share)], pout, mout, 0),
@@ -862,8 +919,6 @@
         wide, lambda b: pkv.at[b], ikv, it_s.at[3], it_r.at[3],
         mates_of(lambda w: gkv.at[tile(w, wide_share), :], pkv, mkv, 2),
     )
-    out.mates.start()
-
     def their_rows(b):
         return lambda block: pl.ds(pl.multiple_of(b * rows + block * share, share), share)
 
@@ -895,22 +950,15 @@
     gather3 = [gather_of(b, layer_ref, 0) for b in range(2)]
     gather4 = [gather_of(b, grad_ref, 1) for b in range(2)]
 
-    loads[1].wait()
     for b in range(2):
-        mine = pl.ds(b * rows, rows)
-
-        def feed(c, carry):
-            part3[mine, tile(c, 512)] = dot_nn(mixed_ref[mine, :], wd[:, tile(c, 512)]).astype(bf16)
-            return carry
-
-        lax.fori_loop(0, width // 512, feed, 0)
         sums3[b].start()
-    loads[2].wait()
-    up.tree.start()
+    for i, item in ((2, up), (6, gate)):
+        loads[i].wait()
+        item.tree.start()
+    loads[7].wait()
+    out.mates.start()
     loads[0].wait()
     stack_rows = heads * half
-    parts = 2
-    part_rows = stack_rows // parts
 
     def attention(b, g):
         length = len_ref[b]
@@ -919,32 +967,23 @@
         held = (dob_ref[pl.ds(b * rows, half), :] if g == 0 else dm[b]).astype(f32)
         stack = head_stack(held, heads, True)
         dos[...] = stack.astype(bf16)
-        for p in range(parts):
-            at = pl.ds(p * part_rows, part_rows)
-            product = stack[p * part_rows : (p + 1) * part_rows] * os_ref[b, g, at, :]
-            delta[:, at] = jnp.sum(jnp.transpose(product), axis=0, keepdims=True)
+        delta[...] = jnp.sum(jnp.transpose(stack * os_ref[b, g]), axis=0, keepdims=True)
         lane = lax.broadcasted_iota(jnp.int32, qclean.shape, 1)
         qclean[...] = jnp.where(lane < HD, qs_ref[b, g].astype(f32), 0.0).astype(bf16)
+        both = jnp.concatenate([qclean[...], dos[...]], axis=0)
         dqacc[...] = jnp.zeros(dqacc.shape, f32)
 
         def step(masked, j, carry):
             block, scored = key_block(kv, j, b, length)
+            scores = dot_nt(scored, qs_ref[b, g])
             if masked:
-                shape = (2 * rows, part_rows)
-                key = 2 * rows * j + lax.broadcasted_iota(jnp.int32, shape, 0)
-                place = first + lax.rem(lax.broadcasted_iota(jnp.int32, shape, 1), half)
-                allowed = key <= place
-            total = acc[j]
-            for p in range(parts):
-                at = pl.ds(p * part_rows, part_rows)
-                scores = dot_nt(scored, qs_ref[b, g, at, :])
-                if masked:
-                    scores = jnp.where(allowed, scores, masked_score)
-                chances = jnp.exp(scores - log_ref[pl.ds(2 * b + g, 1), at])
-                slope = (chances * (dot_nt(block, dos[at, :]) - delta[:, at])).astype(bf16)
-                total = total + dot_nn(slope, qclean[at, :]) + dot_nn(chances.astype(bf16), dos[at, :])
-                dqacc[at, :] = dqacc[at, :] + dot_tn(slope, block)
-            acc[j] = total
+                key = 2 * rows * j + lax.broadcasted_iota(jnp.int32, scores.shape, 0)
+                place = first + lax.rem(lax.broadcasted_iota(jnp.int32, scores.shape, 1), half)
+                scores = jnp.where(key <= place, scores, masked_score)
+            chances = jnp.exp(scores - log_ref[pl.ds(2 * b + g, 1), :])
+            slope = (chances * (dot_nt(block, dos[...]) - delta[...])).astype(bf16)
+            acc[j] = acc[j] + dot_nn(jnp.concatenate([slope, chances.astype(bf16)], axis=1), both)
+            dqacc[...] = dqacc[...] + dot_tn(slope, block)
             return carry
 
         lax.fori_loop(0, final, functools.partial(step, False), 0)
@@ -1044,8 +1083,7 @@
         grad_ref[mine_in(b), :] = (
             dh_ref[b] + inverse * (weighted - z1 * jnp.mean(weighted * z1, axis=-1, keepdims=True))
         ).astype(bf16)
-        gather4[b].start()
-        return jnp.sum(total * z1, axis=0, keepdims=True)
+        grow[pl.ds(b, 1), :] = jnp.sum(total * z1, axis=0, keepdims=True)
 
     clear()
     for copy in grads_there:
@@ -1060,11 +1098,15 @@
     attention(1, 1)
     query_back(1).start()
     pair_mid(0)
+    loads[8].wait()
     result_rows(0)
     result_rows(1)
+    up.relay()
     attention(1, 0)
     pair_send(1)
     pair_relay(0)
+    loads[9].wait()
+    loads[10].wait()
     pair_mid(1)
     pair_total(0)
     query_back(0).wait_recv()
@@ -1091,72 +1133,101 @@
 
     query.mates.add()
     query.tree.start()
+    gate.relay()
     out.mates.add()
     out.tree.start()
     lax.fori_loop(0, width // span, grad_keyval, 0)
     keyval.mates.start()
-    up.relay()
     loads[4].wait()
     loads[5].wait()
-    gain1 = input_rows(0)
+    loads[11].wait()
+    input_rows(0)
+    gather4[0].start()
     keyval.mates.add()
     keyval.tree.start()
     sums4[1].relay(adder(1, part4, into4))
     query.relay()
     out.relay()
+    squares = squares_ref[0:1, 0:1] + up.finish(up_ref) + gate.finish(gate_ref)
     gather4[0].relay()
     keyval.relay()
-    squares = squares_ref[0:1, 0:1] + up.finish(up_ref)
-    gain1 = gain1 + input_rows(1)
-
-    row = lax.broadcasted_iota(jnp.int32, gpart.shape, 0)
-    gain2 = gain2_ref[0:1, :] + gain2_ref[1:2, :]
-    gpart[...] = jnp.where(row == 0, gain1, jnp.where(row == 1, gain2, 0.0))
+
+    input_rows(1)
+    for w in range(16):
+        lanes = pl.ds(w * wide_share, wide_share)
+        gpart[pl.ds(w, 1), :] = grow[0:1, lanes] + grow[1:2, lanes]
+        gpart[pl.ds(16 + w, 1), :] = gain2_ref[0:1, lanes] + gain2_ref[1:2, lanes]
+    near_gains = [
+        remote(gpart, gnear.at[i], h_s.at[0, i], h_r.at[0, i], there)
+        for i, there in enumerate(others_of("narrow"))
+    ]
+    for copy in near_gains:
+        copy.start()
+    gather4[1].start()
+    squares = squares + query.finish(q_ref) + out.finish(out_ref) + keyval.finish(pair)
+    spart[...] = jnp.broadcast_to(squares, spart.shape)
+    near_squares = [
+        remote(spart, snear.at[i], h_s.at[1, i], h_r.at[1, i], there)
+        for i, there in enumerate(others_of("narrow"))
+    ]
+    for copy in near_squares:
+        copy.start()
+    pair_ref[...] = jnp.transpose(pair[...])
+    for b in range(2):
+        gather3[b].arrive()
+    layer_store = pltpu.make_async_copy(layer_ref, layer_hbm, out_sem.at[0])
+    layer_store.start()
+    for copy in near_gains:
+        copy.wait()
+    total = gpart[pl.ds(0, 32), :]
+    for i in range(peers - 1):
+        total = total + gnear[i, pl.ds(0, 32), :]
+    for copy in near_squares:
+        copy.wait()
+    square = spart[...]
+    for i in range(peers - 1):
+        square = square + snear[i]
+    gpart[pl.ds(0, 32), :] = total
+    gpart[pl.ds(32, 8), :] = square
     gain_copies = [
-        remote(gpart.at[:, tile(there[0], wide_share)], gin.at[i], g_s.at[i], g_r.at[i], there)
+        remote(gpart, gwide.at[i], g_s.at[i], g_r.at[i], there)
         for i, there in enumerate(others_of("wide"))
     ]
     for copy in gain_copies:
         copy.start()
-    squares = squares + query.finish(q_ref) + out.finish(out_ref)
-    share_kv = keyval.finish(pair)
-    pair_ref[...] = jnp.transpose(pair[...])
-    squares = squares + share_kv
     gather4[1].relay()
     for copy in gain_copies:
         copy.wait()
-    total = gpart[:, tile(wide_me, wide_share)]
+    total = gpart[...]
     for i in range(len(gain_copies)):
-        total = total + gin[i]
+        total = total + gwide[i]
+    gpart[...] = total
     row = lax.broadcasted_iota(jnp.int32, total.shape, 0)
-    near_own[...] = jnp.where(row < 2, total, jnp.broadcast_to(squares, total.shape))
-    exchange(lambda index: near_own, near, "narrow", h_s, h_r)
-    total = near_own[...]
-    for i in range(peers - 1):
-        total = total + near[i]
-    gains_out_ref[...] = total
-    kept = jnp.where(row < 2, total, 0.0)
+    kept = jnp.where(row < 32, total, 0.0)
     gain_squares = jnp.sum(jnp.sum(kept * kept, axis=1, keepdims=True), axis=0, keepdims=True)
-    norm_own[...] = total[2:3, :] + jnp.broadcast_to(gain_squares, norm_own.shape)
-    exchange(lambda index: norm_own, norm_in, "wide", w_s, w_r)
-    total = norm_own[...]
-    for i in range(len(gain_copies)):
-        total = total + norm_in[i]
-    norm_ref[...] = jnp.sqrt(total)
+    norm_ref[...] = jnp.sqrt(total[32:40, :] + gain_squares)
+    row = lax.broadcasted_iota(jnp.int32, gains_out_ref.shape, 0)
+    gains_out_ref[...] = jnp.where(
+        row == 0, gpart[pl.ds(wide_me, 1), :], gpart[pl.ds(16 + wide_me, 1), :]
+    )
     for b in range(2):
-        gather3[b].arrive()
         gather4[b].arrive()
+    grad_store = pltpu.make_async_copy(grad_ref, grad_hbm, out_sem.at[1])
+    grad_store.start()
+    for b in range(2):
         for each in (sums3[b], sums4[b], gather3[b], gather4[b], pair_mates[b], pair_trees[b]):
             each.drain()
         grads_there[b].wait_send()
         query_back(b).wait_send()
-    for item in (up, out, query, keyval):
+    for item in (gate, up, out, query, keyval):
         item.drain()
+    layer_store.wait()
+    grad_store.wait()
 
 
 def backward(
-    lengths, tokens, gains, wq, wkv, cosine, sine, qs, outs, logs, hidden, mixed, dh, gain2,
-    dob, gout, squares, kv, n1, wd, pup,
+    lengths, gains, tables, logs, mixed, gain2, dob, squares, qs, outs, tokens, wq, wkv, hidden, dh, gout,
+    kv, n1, wd, pgate, pup,
 ):
     count, width = n1.shape
     rows = count // 2
@@ -1172,24 +1243,35 @@
     dma = pltpu.SemaphoreType.DMA
     vmem = pltpu.VMEM
     blocks = (
-        (wide_share, units), (lanes, wide_share),
-        (wide_share, lanes), (wide_share, 2 * HD),
+        (wide_share, units), (lanes, wide_share), (wide_share, lanes), (wide_share, 2 * HD),
     )
     return pl.pallas_call(
         backward_kernel,
         out_shape=(
-            shape((count, width), bf16),
-            shape((count, width), bf16),
             shape((wide_share, lanes), f32),
             shape((2 * HD, wide_share), f32),
             shape((lanes, wide_share), f32),
             shape((wide_share, units), f32),
+            shape((wide_share, units), f32),
             shape((8, wide_share), f32),
             shape((8, wide_share), f32),
+            shape((count, width), bf16),
+            shape((count, width), bf16),
         ),
-        in_specs=[pl.BlockSpec(memory_space=pltpu.SMEM), anywhere] + [here] * 15 + [anywhere] * 4,
-        out_specs=(here,) * 8,
+        in_specs=[pl.BlockSpec(memory_space=pltpu.SMEM)] + [here] * 13 + [anywhere] * 11,
+        out_specs=(here,) * 7 + (anywhere,) * 2,
         scratch_shapes=[
+            vmem((count, width), bf16),
+            vmem((count, width), bf16),
+            vmem(wq.shape, bf16),
+            vmem(wkv.shape, bf16),
+            vmem(hidden.shape, f32),
+            vmem(dh.shape, f32),
+            vmem(gout.shape, bf16),
+            vmem((rows + rows // 2, 2 * HD), f32),
+            vmem((rows + rows // 2, 2 * HD), f32),
+            vmem(pgate.shape, bf16),
+            vmem((SLOTS, wide_share, units), bf16),
             vmem(kv.shape, bf16),
             vmem((count, width), bf16),
             vmem(wd.shape, bf16),
@@ -1216,13 +1298,14 @@
             vmem((1, stack), f32),
             vmem((stack, 2 * HD), f32),
             vmem((8, width), f32),
-            vmem((wide_count - 1, 8, wide_share), f32),
+            vmem((40, wide_share), f32),
+            vmem((7, 40, wide_share), f32),
+            vmem((wide_count - 1, 40, wide_share), f32),
             vmem((8, wide_share), f32),
             vmem((7, 8, wide_share), f32),
-            vmem((8, wide_share), f32),
-            vmem((wide_count - 1, 8, wide_share), f32),
             vmem((wide_share, 2 * HD), f32),
-            dma((6,)),
+            dma((12,)),
+            dma((2,)),
             dma((2, 2, SLOTS)),
             dma((2, 2, SLOTS)),
             dma((2, 2, SLOTS)),
@@ -1233,24 +1316,22 @@
             dma((2, SLOTS)),
             dma((3, 8)),
             dma((3, 8)),
-            dma((4, SLOTS)),
-            dma((4, SLOTS)),
+            dma((5, SLOTS)),
+            dma((5, SLOTS)),
             dma((2, 2)),
             dma((2, 2)),
             dma((wide_count - 1,)),
             dma((wide_count - 1,)),
-            dma((7,)),
-            dma((7,)),
-            dma((wide_count - 1,)),
-            dma((wide_count - 1,)),
+            dma((2, 7)),
+            dma((2, 7)),
         ],
         compiler_params=pltpu.CompilerParams(
             collective_id=2, has_side_effects=True, vmem_limit_bytes=63 * MB
         ),
         name="backward",
     )(
-        lengths, tokens, gains, wq, wkv, cosine, sine, qs, outs, logs, hidden, mixed, dh,
-        gain2, dob, gout, squares, kv, n1, wd, pup,
+        lengths, gains, *tables, logs, mixed, gain2, dob, squares, qs, outs, tokens, wq, wkv, hidden, dh,
+        gout, kv, n1, wd, pgate, pup,
     )
 
 
@@ -1263,7 +1344,8 @@
     (layer, grad), refs = refs[:2], refs[2:]
     outs, refs = [refs[i * count : (i + 1) * count] for i in range(4)], refs[4 * count :]
     (layer_out, grad_out), refs = refs[:2], refs[2:]
-    gain_outs, refs = refs[:4], refs[4:]
+    gain_outs, norm_out, refs = refs[:4], refs[4], refs[5:]
+    norm_out[0, 0] = norm_ref[0, 0]
     held, refs = [refs[i * count : (i + 1) * count] for i in range(5)], refs[5 * count :]
     rows_held, in_sem, out_sem, copy_sem = refs
     wide_me = lax.axis_index("wide")
@@ -1375,9 +1457,9 @@
 
     return pl.pallas_call(
         body,
-        out_shape=tuple(kept * 4 + [shape(layer.shape, bf16), shape(grad.shape, bf16)] + [small] * 4),
+        out_shape=tuple(kept * 4 + [shape(layer.shape, bf16), shape(grad.shape, bf16)] + [small] * 4 + [shape((1, 1), f32)]),
         in_specs=[here] * 5 + [anywhere] * 23,
-        out_specs=tuple([anywhere] * 22 + [here] * 4),
+        out_specs=tuple([anywhere] * 22 + [here] * 4 + [pl.BlockSpec(memory_space=pltpu.SMEM)]),
         scratch_shapes=[
             *[pltpu.VMEM(block, f32) for block in blocks],
             *[pltpu.VMEM(block, bf16) for block in blocks],
@@ -1420,17 +1502,8 @@
 ):
     bucket_count, row_count, model_width = tokens.shape
     wide_count = lax.axis_size("wide")
-    wide_rank = lax.axis_index("wide")
     token_count = bucket_count * row_count
-    half = row_count // 2
-    mirror_rank = wide_count - 1 - wide_rank
-    positions = jnp.concatenate(
-        [
-            wide_rank * row_count + jnp.arange(row_count, dtype=jnp.int32),
-            mirror_rank * row_count + half + jnp.arange(half, dtype=jnp.int32),
-        ]
-    )
-    cosine, sine = lane_tables(positions)
+    tables = rotation_tables(wide_count, row_count)
     inputs = tokens.reshape(token_count, model_width)
     units = down_weight.shape[0]
 
@@ -1442,16 +1515,16 @@
 
     pair_weight = turned(keyval_weight)
     (
-        normed_one, pairs, query_stack, out_stack, logs, hidden, mixed, grad_hidden, gain_two, grad_heads,
-        output_grad, gate_sum, down_sum, squares, up_part,
+        logs, grad_hidden, gain_two, grad_heads, output_grad, down_sum, squares, normed_one, pairs,
+        query_stack, out_stack, hidden, mixed, gate_part, up_part,
     ) = forward(
-        lengths, inputs, norm_gains, query_weight, pair_weight, cosine, sine, output_weight,
-        gateup_weight, down_weight, cotangent.reshape(token_count, model_width),
-    )
-    layer_rows, grad_rows, query_sum, pair_sum, output_sum, up_sum, gains_sum, norm = backward(
-        lengths, inputs, norm_gains, query_weight, pair_weight, cosine, sine, query_stack, out_stack,
-        logs, hidden, mixed, grad_hidden, gain_two, grad_heads, output_grad, squares, pairs, normed_one,
-        down_weight, up_part,
+        lengths, inputs, norm_gains, pair_weight, tables, query_weight, output_weight, gateup_weight,
+        down_weight, cotangent.reshape(token_count, model_width),
+    )
+    query_sum, pair_sum, output_sum, gate_sum, up_sum, gains_sum, norm, layer_rows, grad_rows = backward(
+        lengths, norm_gains, tables, logs, mixed, gain_two, grad_heads, squares, query_stack, out_stack,
+        inputs, query_weight, pair_weight, hidden, grad_hidden, output_grad, pairs, normed_one, down_weight,
+        gate_part, up_part,
     )
     results = update(
         norm, gains_sum, norm_gains, gains_first, gains_second,
@@ -1469,7 +1542,7 @@
         kinds.append((query, turned_back(pair), output, gateup, down, results[22 + kind]))
     clipped, momentum, variance, updated = kinds
     return (
-        layer_out, input_grad, *clipped, norm[0, 0], *momentum, *variance, *updated,
+        layer_out, input_grad, *clipped, results[26].reshape(()), *momentum, *variance, *updated,
     )
 
 

time: 257 us -> 241 us (0.938)
  Pallas kernels: 253 us -> 238 us
    pallas_call x2, Pallas kernels: 243 us -> 228 us  [the longest x1 122 us: forward(): pl.pallas_call(forward_kernel, out_shape=(shape((8, stack), f32), shape((...]
where the time goes in v1:
time: 241 us; the launch traced here: 239 us
  Pallas kernels  238 us (99%)
    pallas_call x1, Pallas kernels, forward(): pl.pallas_call(forward_kernel, out_shape=(shape((8, stack), f32), shape((...  122 us
    pallas_call x1, Pallas kernels, backward(): pl.pallas_call(backward_kernel, out_shape=(shape((wide_share, lanes), f32...  107 us
    pallas_call x1, Pallas kernels, update(): pl.pallas_call(body, out_shape=tuple(kept * 4 + [shape(layer.shape, bf16)...  9.93 us

profile of v1, /device:TPU:1, one launch (start us, length us, event | category | flops | bytes accessed | tf_op | source)
XLA Modules:
  0.0 239.1 jit_solution(18257448991630730848)
XLA Ops:
  0.7 121.8 %forward.1 = (f32[8,512]{1,0:T(8,128)}, f32[2,32,2048]{2,1,0:T(8,128)}, f32[8,2048]{1,0:T(8,128)}, bf16[512,256]{1,0:T(8,128)(2,1)}, bf16[256,2048]{1,0:T(8,128)...) custom-call(s32[2]{0:T(128)} %len_ref.3, ...), custom_call_target="tpu_custom_call" | custom-call | tf_op jit(solution)/shard_map/forward/pallas_call | solution.py:765
  122.4 106.5 %backward.1 = (f32[128,256]{1,0:T(8,128)}, f32[128,128]{1,0:T(8,128)}, f32[256,128]{1,0:T(8,128)}, f32[128,1024]{1,0:T(8,128)}, f32[128,1024]{1,0:T(8,128)}, /*i...) custom-call(s32[2]{0:T(128)} %len_ref.3, bf16[2,2048]{1,0:T(2,128)(2,1)} %refs_2_.1, ...), custom_call_target="tpu_custom_call" | custom-call | tf_op jit(solution)/shard_map/backward/pallas_call | solution.py:1248
  229.0 9.9 %update.1 = (f32[1024,128]{1,0:T(8,128)}, f32[2,128,1024]{2,1,0:T(8,128)}, f32[256,128]{1,0:T(8,128)}, f32[128,256]{1,0:T(8,128)}, f32[128,128]{1,0:T(8,128)}, /...) custom-call(f32[8,128]{1,0:T(8,128)} %get-tuple-element.92.refs_0_, ...), custom_call_target="tpu_custom_call" | custom-call | tf_op jit(solution)/shard_map/update/pallas_call | solution.py:1458

commit v2 on v1

--- a/solution.py
+++ b/solution.py
@@ -33,6 +33,7 @@
 MESH = pl.DeviceIdType.MESH
 MB = 1024 * 1024
 SLOTS = 7
+EARLY = (0,)
 
 
 def rotation_tables(wide_count, row_count):
@@ -156,75 +157,119 @@
     return (lax.axis_size("wide") - 1 - lax.axis_index("wide"), lax.axis_index("narrow"))
 
 
-class TreeSum:
-    first = (((1, 1), (0, 1)), ((1, -1), (0, -1)), ((1, 2), (1, 0)), ((0, 1), (0, 1)), ((0, -1), (0, -1)))
-    second = (((1, 0), (1, 0)), ((0, 2), (0, 2)))
-
+class Relay:
+    def __init__(self, grid, ssem, rsem):
+        self.grid, self.ssem, self.rsem = grid, ssem, rsem
+
+    def copy(self, i):
+        block, there = self.routes[i]
+        src, dst = self.source(self.grid.block(*block)), self.target(i, self.grid.block(*block))
+        return remote(src, dst, self.ssem.at[i], self.rsem.at[i], self.grid.device(*there))
+
+    def send(self, *numbers):
+        for i in numbers:
+            self.copy(i).start()
+
+    def take(self, *numbers):
+        for i in numbers:
+            self.copy(i).wait_recv()
+
+    def drain(self, numbers=range(7)):
+        for i in numbers:
+            self.copy(i).wait_send()
+
+
+class SumRelay(Relay):
     def __init__(self, grid, part, into, ssem, rsem):
-        self.grid, self.part, self.into, self.ssem, self.rsem = grid, part, into, ssem, rsem
-
-    def copy(self, slot):
-        block, there = (self.first + self.second)[slot]
-        return remote(
-            self.part(self.grid.block(*block)), self.into(slot), self.ssem.at[slot],
-            self.rsem.at[slot], self.grid.device(*there),
-        )
+        super().__init__(grid, ssem, rsem)
+        self.source, self.into = part, into
+
+    def target(self, i, block):
+        return self.into(self.slots[i])
+
+    def add(self, block, slots):
+        ref = self.source(self.grid.block(*block))
+        total = ref[...].astype(f32)
+        for slot in slots:
+            total = total + self.into(slot)[...].astype(f32)
+        ref[...] = total.astype(ref.dtype)
+
+    def total(self, rows):
+        total = self.source(self.grid.block(0, 0))[rows, :].astype(f32)
+        for slot in self.final:
+            total = total + self.into(slot)[rows, :].astype(f32)
+        return total
+
+
+class FarSum(SumRelay):
+    routes = (
+        ((1, 1), (0, 1)), ((1, -1), (0, -1)), ((1, 2), (1, 0)),
+        ((0, 1), (0, 1)), ((0, -1), (0, -1)), ((1, 0), (1, 0)), ((0, 2), (0, 2)),
+    )
+    slots = (0, 1, 2, 3, 4, 5, 6)
+    final = (3, 4, 5, 6)
 
     def start(self):
-        for slot in range(5):
-            self.copy(slot).start()
-
-    def relay(self, add):
-        self.copy(0).wait_recv()
-        self.copy(1).wait_recv()
-        add(self.grid.block(1, 0), (0, 1))
-        self.copy(5).start()
-        self.copy(2).wait_recv()
-        add(self.grid.block(0, 2), (2,))
-        self.copy(6).start()
+        self.send(0, 1, 2, 3, 4)
+
+    def relay(self, taken=False):
+        if not taken:
+            self.take(0, 1)
+        self.add((1, 0), (0, 1))
+        self.send(5)
+        if not taken:
+            self.take(2)
+        self.add((0, 2), (2,))
+        self.send(6)
+
+    def arrive(self, taken=False):
+        self.take(*((5, 6) if taken else (3, 4, 5, 6)))
+
+
+class CrossSum(SumRelay):
+    routes = (
+        ((1, 1), (0, 1)), ((1, -1), (0, -1)), ((1, 2), (0, 2)),
+        ((0, 1), (0, 1)), ((0, -1), (0, -1)), ((0, 2), (0, 2)), ((1, 0), (1, 0)),
+    )
+    slots = (0, 1, 2, 3, 4, 5, 6)
+    final = (3, 4, 5, 6)
+
+    def start(self):
+        self.send(0, 1, 2, 3, 4, 5)
+
+    def relay(self):
+        self.take(0, 1, 2)
+        self.add((1, 0), (0, 1, 2))
+        self.send(6)
 
     def arrive(self):
-        for slot in (3, 4, 5, 6):
-            self.copy(slot).wait_recv()
-
-    def drain(self):
-        for slot in range(SLOTS):
-            self.copy(slot).wait_send()
-
-
-class TreeGather:
-    plan = (
+        self.take(3, 4, 5, 6)
+
+
+class FarGather(Relay):
+    routes = (
         ((0, 0), (1, 0)), ((0, 0), (0, 1)), ((0, 0), (0, -1)), ((0, 0), (0, 2)),
         ((1, 0), (0, 1)), ((1, 0), (0, -1)), ((0, 2), (1, 0)),
     )
-    lands = ((1, 0), (0, -1), (0, 1), (0, 2), (1, -1), (1, 1), (1, 2))
 
     def __init__(self, grid, place, ssem, rsem):
-        self.grid, self.place, self.ssem, self.rsem = grid, place, ssem, rsem
-
-    def copy(self, slot):
-        block, there = self.plan[slot]
-        ref = self.place(self.grid.block(*block))
-        return remote(ref, ref, self.ssem.at[slot], self.rsem.at[slot], self.grid.device(*there))
+        super().__init__(grid, ssem, rsem)
+        self.source = place
+
+    def target(self, i, block):
+        return self.source(block)
 
     def start(self):
-        for slot in range(4):
-            self.copy(slot).start()
+        self.send(0, 1, 2, 3)
 
     def relay(self):
-        self.copy(0).wait_recv()
-        self.copy(4).start()
-        self.copy(5).start()
-        self.copy(3).wait_recv()
-        self.copy(6).start()
+        self.take(0)
+        self.send(4, 5)
+        self.take(3)
+        self.send(6)
 
     def arrive(self):
-        for slot in (1, 2, 4, 5, 6):
-            self.copy(slot).wait_recv()
-
-    def drain(self):
-        for slot in range(SLOTS):
-            self.copy(slot).wait_send()
+        self.take(1, 2, 4, 5, 6)
 
 
 class MateSum:
@@ -290,25 +335,10 @@
     return jnp.where(lane < HD, even, pltpu.roll(odd, HD, 1))
 
 
-def block_adder(part, into):
-    def add(block, slots):
-        total = part(block)[...].astype(f32)
-        for slot in slots:
-            total = total + into(slot)[...].astype(f32)
-        part(block)[...] = total.astype(part(block).dtype)
-
-    return add
-
-
 class Item:
-    def __init__(self, grid, part, into, ssem, rsem, mates=None):
-        self.part, self.into, self.mates = part, into, mates
-        self.own = grid.block(0, 0)
-        self.tree = TreeSum(grid, part, lambda slot: into.at[slot], ssem, rsem)
-        self.add = block_adder(part, lambda slot: into.at[slot])
-
-    def relay(self):
-        self.tree.relay(self.add)
+    def __init__(self, tree, grid, part, into, ssem, rsem, mates=None):
+        self.tree = tree(grid, part, lambda slot: into.at[slot], ssem, rsem)
+        self.mates = mates
 
     def finish(self, out_ref):
         self.tree.arrive()
@@ -317,9 +347,7 @@
 
         def per_tile(j, squares):
             rows = tile(j, span)
-            total = self.part(self.own)[rows, :].astype(f32)
-            for slot in (3, 4, 5, 6):
-                total = total + self.into[slot, rows, :].astype(f32)
+            total = self.tree.total(rows)
             out_ref[rows, :] = total
             return squares + jnp.sum(total * total, axis=0, keepdims=True)
 
@@ -356,7 +384,7 @@
     len_ref, tok_ref, gains_ref, wkv_ref, tab0, tab1, tab2, tab3, tab4, wq_hbm, wo_hbm, wgu_hbm, wd_hbm,
     cot_hbm,
     log_ref, dh_ref, gain_ref, dob_ref, gout_ref, down_ref, squares_ref,
-    n1_hbm, kv_hbm, qs_hbm, os_hbm, hidden_hbm, mixed_hbm, pgate_hbm, pup_hbm,
+    n1_hbm, kv_hbm, qs_hbm, os_hbm, hidden_hbm, part_hbm, into_hbm, pgate_hbm, pup_hbm,
     wq_ref, qs_ref, os_ref, hidden_ref, mixed_ref,
     wo, wgu, wd, dyb, n1, kv, q, qm, ob, om, da, n2, dgu, dhb, part1, part2, into1, into2,
     mate_gu, mate_d, gdn, idown,
@@ -404,15 +432,14 @@
         bucket = pl.ds(b * rows, rows)
         return lambda block: kv.at[2 * block + core, bucket, :]
 
-    keys = [TreeGather(wide, keys_at(b), kv_s.at[b], kv_r.at[b]) for b in range(2)]
+    keys = [FarGather(wide, keys_at(b), kv_s.at[b], kv_r.at[b]) for b in range(2)]
 
     def to_mate(b, block, i):
         ref = keys_at(b)(block)
         return remote(ref, ref, km_s.at[b, i], km_r.at[b, i], mate)
 
-    for b in range(2):
-        keys[b].start()
-        to_mate(b, chip, 7).start()
+    keys[0].start()
+    to_mate(0, chip, 7).start()
     loads[4].wait()
     for pair in range(heads // 2):
         columns = pl.ds(pair * 2 * HD, 2 * HD)
@@ -460,17 +487,26 @@
     for b in range(2):
         stack_queries(b, 0)
     keys_relay(0)
+    keys[1].start()
+    to_mate(1, chip, 7).start()
     loads[1].wait()
     for b in range(2):
         place = wide_me * rows + lax.broadcasted_iota(jnp.int32, (rows, 1), 0)
         mine = pl.ds(b * rows, rows)
         live = (place < len_ref[b]).astype(f32)
         dyb[mine, :] = (dyb[mine, :].astype(f32) * live).astype(bf16)
-    keys_relay(1)
+    loads[2].wait()
+
+    def grad_middle(j, carry):
+        da[:, tile(j, span)] = dot_nt(dyb[...], wd[tile(j, span), :])
+        return carry
+
+    lax.fori_loop(0, units // span, grad_middle, 0)
     for b in range(2):
         queries[b].wait_recv()
         stack_queries(b, 1)
     keys_arrive(0)
+    keys_relay(1)
 
     stack_rows = heads * half
 
@@ -522,36 +558,21 @@
 
     def sum_of(b, part, into, number):
         where = their_rows(b)
-        return TreeSum(
+        return FarSum(
             narrow, lambda block: part.at[where(block), :], lambda slot: into.at[b, slot],
             rs_s.at[number, b], rs_r.at[number, b],
         )
 
-    def adder(b, part, into):
-        where = their_rows(b)
-
-        def add(block, slots):
-            total = part[where(block), :].astype(f32)
-            for slot in slots:
-                total = total + into[b, slot].astype(f32)
-            part[where(block), :] = total.astype(bf16)
-
-        return add
-
-    def total_of(b, part, into):
-        total = part[mine_in(b), :].astype(f32)
-        for slot in (3, 4, 5, 6):
-            total = total + into[b, slot].astype(f32)
-        return total
-
     def gather_of(b, buffer, number):
         where = their_rows(b)
-        return TreeGather(
+        return FarGather(
             narrow, lambda block: buffer.at[where(block), :], ag_s.at[number, b], ag_r.at[number, b]
         )
 
+    whole = pl.ds(0, share)
     sums1 = [sum_of(b, part1, into1, 0) for b in range(2)]
     sums2 = [sum_of(b, part2, into2, 1) for b in range(2)]
+    sums3 = [sum_of(b, part1, into1, 2) for b in range(2)]
     gather1 = [gather_of(b, n2, 0) for b in range(2)]
     gather2 = [gather_of(b, dhb, 1) for b in range(2)]
 
@@ -576,21 +597,14 @@
     store(os_ref, os_hbm, 2).start()
     store(qs_ref, qs_hbm, 3).start()
     project(1)
-    sums1[0].relay(adder(0, part1, into1))
-    loads[2].wait()
-
-    def grad_middle(j, carry):
-        da[:, tile(j, span)] = dot_nt(dyb[...], wd[tile(j, span), :])
-        return carry
-
-    lax.fori_loop(0, units // span, grad_middle, 0)
-    sums1[1].relay(adder(1, part1, into1))
+    sums1[0].relay()
+    sums1[1].relay()
     gain2 = gains_ref[1:2, :].astype(f32)
     gain_ref[...] = jnp.zeros(gain_ref.shape, f32)
 
     def second_norm(b):
         sums1[b].arrive()
-        hidden = tok_ref[mine_in(b), :].astype(f32) + total_of(b, part1, into1)
+        hidden = tok_ref[mine_in(b), :].astype(f32) + sums1[b].total(whole)
         hidden_ref[b] = hidden
         n2[mine_in(b), :] = (hidden * inverse_rms(hidden) * gain2).astype(bf16)
         gather1[b].start()
@@ -634,7 +648,6 @@
     feed(0)
     feed(1)
     store(hidden_ref, hidden_hbm, 4).start()
-    store(mixed_ref, mixed_hbm, 5).start()
     wide_share = width // 16
     mates = [
         MateSum(
@@ -650,7 +663,9 @@
             mt_s.at[2], mt_r.at[2],
         )
     )
-    down = Item(wide, mates[2].own, idown, it_s, it_r, mates[2])
+    down = Item(
+        CrossSum, wide, mates[2].own, idown, it_s, it_r, mates[2]
+    )
 
     def grad_down(j, carry):
         found = dot_tn(mixed_ref[:, tile(j, span)], dyb[...]).astype(bf16)
@@ -667,7 +682,7 @@
 
     def second_norm_back(b):
         sums2[b].arrive()
-        total = total_of(b, part2, into2)
+        total = sums2[b].total(whole)
         hidden = hidden_ref[b]
         inverse = inverse_rms(hidden)
         z2 = hidden * inverse
@@ -692,36 +707,51 @@
 
         lax.fori_loop(0, 8, per_block, 0)
 
+    def feed_down(c, carry):
+        part1[:, tile(c, 512)] = dot_nn(mixed_ref[...], wd[:, tile(c, 512)]).astype(bf16)
+        return carry
+
+    def grad_heads(b):
+        gather2[b].arrive()
+        mine = pl.ds(b * rows, rows)
+        dob_ref[mine, :] = dot_nt(dhb[mine, :], wo[...]).astype(bf16)
+
+    def grad_out(j, carry):
+        gout_ref[:, tile(j, span)] = dot_tn(ob[...], dhb[:, tile(j, span)]).astype(bf16)
+        return carry
+
+    sums2[0].relay()
     lax.fori_loop(0, units // span, grad_down, 0)
     mates[2].start()
-    sums2[0].relay(adder(0, part2, into2))
     grad_gateup(0)
+    mates[0].start()
+    sums2[1].relay()
+    second_norm_back(0)
     mates[2].add()
     down.tree.start()
-    mates[0].start()
-    sums2[1].relay(adder(1, part2, into2))
-    second_norm_back(0)
+    sums1[0].drain()
+    sums1[1].drain()
+    lax.fori_loop(0, width // 512, feed_down, 0)
     second_norm_back(1)
     gather2[0].relay()
+    store(part1, part_hbm, 5).start()
     grad_gateup(1)
     mates[1].start()
     gather2[1].relay()
-    down.relay()
+    for b in EARLY:
+        sums3[b].start()
     keep(0, pgate_hbm)
-    for b in range(2):
-        gather2[b].arrive()
-        mine = pl.ds(b * rows, rows)
-        dob_ref[mine, :] = dot_nt(dhb[mine, :], wo[...]).astype(bf16)
-
-    def grad_out(j, carry):
-        gout_ref[:, tile(j, span)] = dot_tn(ob[...], dhb[:, tile(j, span)]).astype(bf16)
-        return carry
-
+    down.tree.relay()
+    grad_heads(0)
+    grad_heads(1)
     lax.fori_loop(0, width // span, grad_out, 0)
     keep(1, pup_hbm)
     squares_ref[...] = jnp.broadcast_to(down.finish(down_ref), squares_ref.shape)
+    for b in EARLY:
+        sums3[b].take(0, 1, 2, 3, 4)
+        sums3[b].drain(range(5))
+        store(into1.at[b, pl.ds(0, 5)], into_hbm.at[b], 6 + b).start()
     for b in range(2):
-        sums1[b].drain()
         sums2[b].drain()
         gather1[b].drain()
         gather2[b].drain()
@@ -736,9 +766,11 @@
     mates[1].drain()
     for i, (src, dst) in enumerate(
         ((n1, n1_hbm), (kv, kv_hbm), (os_ref, os_hbm), (qs_ref, qs_hbm), (hidden_ref, hidden_hbm),
-         (mixed_ref, mixed_hbm))
+         (part1, part_hbm))
     ):
         store(src, dst, i).wait()
+    for b in EARLY:
+        store(into1.at[b, pl.ds(0, 5)], into_hbm.at[b], 6 + b).wait()
     for which, out_hbm in ((0, pgate_hbm), (1, pup_hbm)):
         def per_store(k, carry):
             kept(which, out_hbm, k).wait()
@@ -777,12 +809,13 @@
             shape((2, 2, stack, 2 * HD), bf16),
             shape((2, 2, stack, 2 * HD), f32),
             shape((2, share, width), f32),
-            shape((count, units), bf16),
+            shape((count, width), bf16),
+            shape((2, 5, share, width), bf16),
             shape((8, wide_share, units), bf16),
             shape((8, wide_share, units), bf16),
         ),
         in_specs=[pl.BlockSpec(memory_space=pltpu.SMEM)] + [here] * 8 + [anywhere] * 5,
-        out_specs=(here,) * 7 + (anywhere,) * 8,
+        out_specs=(here,) * 7 + (anywhere,) * 9,
         scratch_shapes=[
             vmem(wq.shape, bf16),
             vmem((2, 2, stack, 2 * HD), bf16),
@@ -812,7 +845,7 @@
             vmem((wide_count, units, wide_share), bf16),
             vmem((SLOTS, units, wide_share), bf16),
             dma((5,)),
-            dma((6,)),
+            dma((8,)),
             dma((2, 8)),
             dma((2, SLOTS)),
             dma((2, SLOTS)),
@@ -820,8 +853,8 @@
             dma((2, 8)),
             dma((2, 2)),
             dma((2, 2)),
-            dma((2, 2, SLOTS)),
-            dma((2, 2, SLOTS)),
+            dma((3, 2, SLOTS)),
+            dma((3, 2, SLOTS)),
             dma((2, 2, SLOTS)),
             dma((2, 2, SLOTS)),
             dma((3, 8)),
@@ -837,14 +870,14 @@
 
 
 def backward_kernel(
-    len_ref, gains_ref, tab0, tab1, tab2, tab3, tab4, log_ref, mixed_ref, gain2_ref, dob_ref, squares_ref,
-    qs_ref, os_ref, tok_hbm, wq_hbm, wkv_hbm, hidden_hbm, dh_hbm, gout_hbm, kv_hbm, n1_hbm, wd_hbm,
+    len_ref, gains_ref, tab0, tab1, tab2, tab3, tab4, log_ref, gain2_ref, dob_ref, squares_ref,
+    qs_ref, os_ref, tok_hbm, wq_hbm, wkv_hbm, hidden_hbm, dh_hbm, gout_hbm, kv_hbm, n1_hbm, part_hbm, into_hbm,
     pgate_hbm, pup_hbm,
     q_ref, pair_ref, out_ref, gate_ref, up_ref, gains_out_ref, norm_ref, layer_hbm, grad_hbm,
     layer_ref, grad_ref, wq_ref, wkv_ref, hidden_ref, dh_ref, gout_ref, cos_ref, sin_ref, pgate, igate,
-    kv, n1, wd, tok, pup, pout, pq, pkv, iup, iout, iq, ikv,
+    kv, n1, tok, pup, pout, pq, pkv, iup, iout, iq, ikv,
     mout, mq, mkv, gq, gkv, part3, part4, into3, into4, acc, dkv, dkm, dkin, dkv_low, dq, dqm, dm,
-    dos, qclean, delta, dqacc, grow, gpart, gnear, gwide, spart, snear, pair,
+    dos, qclean, delta, dqacc, grow, gpart, gnear, gwide, pair,
     ld_sem, out_sem, rs_s, rs_r, ag_s, ag_r, dm_s, dm_r, dt_s, dt_r, im_s, im_r, it_s, it_r, ex_s, ex_r,
     g_s, g_r, h_s, h_r,
 ):
@@ -870,28 +903,23 @@
         return pl.ds(b * rows + half, half)
 
     moves = (
-        (kv_hbm, kv), (wd_hbm, wd), (pup_hbm, pup), (n1_hbm, n1),
+        (kv_hbm, kv), (part_hbm, part3), (pup_hbm, pup), (n1_hbm, n1),
         (tok_hbm.at[mine_in(0), :], tok.at[0]), (tok_hbm.at[mine_in(1), :], tok.at[1]),
         (pgate_hbm, pgate), (gout_hbm, gout_ref), (hidden_hbm, hidden_ref), (wq_hbm, wq_ref),
-        (wkv_hbm, wkv_ref), (dh_hbm, dh_ref),
+        (wkv_hbm, wkv_ref), (dh_hbm, dh_ref), (into_hbm.at[0], into3.at[0, pl.ds(0, 5)]),
+        (into_hbm.at[1], into3.at[1, pl.ds(0, 5)]),
     )
     loads = [pltpu.make_async_copy(src, dst, ld_sem.at[i]) for i, (src, dst) in enumerate(moves)]
     partners = others_of("narrow") + others_of("wide")
     greet(partners)
-    for i in (1, 0, 2, 6, 7, 8, 9, 10, 3, 4, 5, 11):
+    waits_early = [12 + b for b in EARLY]
+    for i in [1] + waits_early + [0, 2, 6, 7, 8, 9, 10, 3, 4, 5, 11]:
         loads[i].start()
     tables = (tab0, tab1, tab2, tab3, tab4)
     cos_ref[pl.ds(0, rows), :], sin_ref[pl.ds(0, rows), :] = rotation(tables, wide_me, 0, rows)
     cos_ref[pl.ds(rows, half), :], sin_ref[pl.ds(rows, half), :] = rotation(
         tables, 2 * last_chip + 1 - wide_me, half, half
     )
-    loads[1].wait()
-
-    def feed(c, carry):
-        part3[:, tile(c, 512)] = dot_nn(mixed_ref[...], wd[:, tile(c, 512)]).astype(bf16)
-        return carry
-
-    lax.fori_loop(0, width // 512, feed, 0)
     met(partners)
 
     grads_there = [
@@ -905,53 +933,49 @@
             source, lambda k: own.at[k], lambda k: into.at[k], im_s.at[number], im_r.at[number]
         )
 
-    up = Item(wide, lambda b: pup.at[b], iup, it_s.at[0], it_r.at[0])
-    gate = Item(wide, lambda b: pgate.at[b], igate, it_s.at[4], it_r.at[4])
+    up = Item(FarSum, wide, lambda b: pup.at[b], iup, it_s.at[0], it_r.at[0])
+    gate = Item(FarSum, wide, lambda b: pgate.at[b], igate, it_s.at[4], it_r.at[4])
     out = Item(
-        wide, lambda b: pout.at[b], iout, it_s.at[1], it_r.at[1],
+        FarSum, wide, lambda b: pout.at[b], iout, it_s.at[1], it_r.at[1],
         mates_of(lambda w: gout_ref.at[:, tile(w, wide_share)], pout, mout, 0),
     )
     query = Item(
-        wide, lambda b: pq.at[b], iq, it_s.at[2], it_r.at[2],
+        FarSum, wide, lambda b: pq.at[b], iq, it_s.at[2], it_r.at[2],
         mates_of(lambda w: gq.at[tile(w, wide_share), :], pq, mq, 1),
     )
     keyval = Item(
-        wide, lambda b: pkv.at[b], ikv, it_s.at[3], it_r.at[3],
+        FarSum, wide, lambda b: pkv.at[b], ikv, it_s.at[3], it_r.at[3],
         mates_of(lambda w: gkv.at[tile(w, wide_share), :], pkv, mkv, 2),
     )
     def their_rows(b):
         return lambda block: pl.ds(pl.multiple_of(b * rows + block * share, share), share)
 
-    def sum_of(b, part, into, number):
+    def sum_of(kind, b, part, into, number):
         where = their_rows(b)
-        return TreeSum(
+        return kind(
             narrow, lambda block: part.at[where(block), :], lambda slot: into.at[b, slot],
             rs_s.at[number, b], rs_r.at[number, b],
         )
 
-    def adder(b, part, into):
+    def gather_of(kind, b, buffer, number):
         where = their_rows(b)
-        return block_adder(lambda block: part.at[where(block), :], lambda slot: into.at[b, slot])
-
-    def total_of(b, part, into):
-        total = part[mine_in(b), :].astype(f32)
-        for slot in (3, 4, 5, 6):
-            total = total + into[b, slot].astype(f32)
-        return total
-
-    def gather_of(b, buffer, number):
-        where = their_rows(b)
-        return TreeGather(
+        return kind(
             narrow, lambda block: buffer.at[where(block), :], ag_s.at[number, b], ag_r.at[number, b]
         )
 
-    sums3 = [sum_of(b, part3, into3, 0) for b in range(2)]
-    sums4 = [sum_of(b, part4, into4, 1) for b in range(2)]
-    gather3 = [gather_of(b, layer_ref, 0) for b in range(2)]
-    gather4 = [gather_of(b, grad_ref, 1) for b in range(2)]
-
+    whole = pl.ds(0, share)
+    sums3 = [sum_of(FarSum, b, part3, into3, 0) for b in range(2)]
+    sums4 = [sum_of(FarSum, b, part4, into4, 1) for b in range(2)]
+    gather3 = [gather_of(FarGather, b, layer_ref, 0) for b in range(2)]
+    gather4 = [gather_of(FarGather, b, grad_ref, 1) for b in range(2)]
+
+    loads[1].wait()
     for b in range(2):
-        sums3[b].start()
+        if b in EARLY:
+            loads[12 + b].wait()
+            sums3[b].relay(taken=True)
+        else:
+            sums3[b].start()
     for i, item in ((2, up), (6, gate)):
         loads[i].wait()
         item.tree.start()
@@ -1018,7 +1042,7 @@
         for b in range(2)
     ]
     pair_trees = [
-        TreeSum(
+        FarSum(
             wide, lambda block, b=b: dkv.at[b, 2 * block + core], lambda slot, b=b: dkin.at[b, slot],
             dt_s.at[b], dt_r.at[b],
         )
@@ -1026,9 +1050,7 @@
     ]
 
     def pair_relay(b):
-        pair_trees[b].relay(
-            block_adder(lambda block: dkv.at[b, 2 * block + core], lambda slot: dkin.at[b, slot])
-        )
+        pair_trees[b].relay()
 
     def pair_send(b):
         def per_block(j, carry):
@@ -1044,9 +1066,7 @@
 
     def pair_total(b):
         pair_trees[b].arrive()
-        total = dkv[b, wide_me].astype(f32)
-        for slot in (3, 4, 5, 6):
-            total = total + dkin[b, slot].astype(f32)
+        total = pair_trees[b].total(pl.ds(0, rows))
         mine = pl.ds(b * rows, rows)
         lane = lax.broadcasted_iota(jnp.int32, total.shape, 1)
         table = pl.ds(0, rows)
@@ -1067,15 +1087,15 @@
         sums4[b].start()
 
     def result_rows(b):
-        sums3[b].arrive()
-        layer_ref[mine_in(b), :] = (hidden_ref[b] + total_of(b, part3, into3)).astype(bf16)
+        sums3[b].arrive(taken=b in EARLY)
+        layer_ref[mine_in(b), :] = (hidden_ref[b] + sums3[b].total(whole)).astype(bf16)
         gather3[b].start()
 
     gains1 = gains_ref[0:1, :].astype(f32)
 
     def input_rows(b):
         sums4[b].arrive()
-        total = total_of(b, part4, into4)
+        total = sums4[b].total(whole)
         values = tok[b].astype(f32)
         inverse = inverse_rms(values)
         z1 = values * inverse
@@ -1086,14 +1106,16 @@
         grow[pl.ds(b, 1), :] = jnp.sum(total * z1, axis=0, keepdims=True)
 
     clear()
+    attention(0, 0)
     for copy in grads_there:
         copy.wait_recv()
     attention(0, 1)
     query_back(0).start()
-    attention(0, 0)
     pair_send(0)
-    sums3[0].relay(adder(0, part3, into3))
-    sums3[1].relay(adder(1, part3, into3))
+    if 0 not in EARLY:
+        sums3[0].relay()
+    if 1 not in EARLY:
+        sums3[1].relay()
     clear()
     attention(1, 1)
     query_back(1).start()
@@ -1101,7 +1123,7 @@
     loads[8].wait()
     result_rows(0)
     result_rows(1)
-    up.relay()
+    up.tree.relay()
     attention(1, 0)
     pair_send(1)
     pair_relay(0)
@@ -1123,7 +1145,7 @@
     pair_relay(1)
     lax.fori_loop(0, width // span, grad_query, 0)
     query.mates.start()
-    sums4[0].relay(adder(0, part4, into4))
+    sums4[0].relay()
     pair_total(1)
     norm_one_back(1)
 
@@ -1133,7 +1155,7 @@
 
     query.mates.add()
     query.tree.start()
-    gate.relay()
+    gate.tree.relay()
     out.mates.add()
     out.tree.start()
     lax.fori_loop(0, width // span, grad_keyval, 0)
@@ -1145,50 +1167,34 @@
     gather4[0].start()
     keyval.mates.add()
     keyval.tree.start()
-    sums4[1].relay(adder(1, part4, into4))
-    query.relay()
-    out.relay()
+    sums4[1].relay()
+    query.tree.relay()
+    out.tree.relay()
     squares = squares_ref[0:1, 0:1] + up.finish(up_ref) + gate.finish(gate_ref)
     gather4[0].relay()
-    keyval.relay()
-
+    keyval.tree.relay()
     input_rows(1)
+    squares = squares + query.finish(q_ref) + out.finish(out_ref) + keyval.finish(pair)
+
     for w in range(16):
         lanes = pl.ds(w * wide_share, wide_share)
         gpart[pl.ds(w, 1), :] = grow[0:1, lanes] + grow[1:2, lanes]
         gpart[pl.ds(16 + w, 1), :] = gain2_ref[0:1, lanes] + gain2_ref[1:2, lanes]
+    gpart[pl.ds(32, 8), :] = jnp.broadcast_to(squares, (8, wide_share))
     near_gains = [
-        remote(gpart, gnear.at[i], h_s.at[0, i], h_r.at[0, i], there)
+        remote(gpart, gnear.at[i], h_s.at[i], h_r.at[i], there)
         for i, there in enumerate(others_of("narrow"))
     ]
     for copy in near_gains:
         copy.start()
     gather4[1].start()
-    squares = squares + query.finish(q_ref) + out.finish(out_ref) + keyval.finish(pair)
-    spart[...] = jnp.broadcast_to(squares, spart.shape)
-    near_squares = [
-        remote(spart, snear.at[i], h_s.at[1, i], h_r.at[1, i], there)
-        for i, there in enumerate(others_of("narrow"))
-    ]
-    for copy in near_squares:
-        copy.start()
     pair_ref[...] = jnp.transpose(pair[...])
-    for b in range(2):
-        gather3[b].arrive()
-    layer_store = pltpu.make_async_copy(layer_ref, layer_hbm, out_sem.at[0])
-    layer_store.start()
     for copy in near_gains:
         copy.wait()
-    total = gpart[pl.ds(0, 32), :]
+    total = gpart[...]
     for i in range(peers - 1):
-        total = total + gnear[i, pl.ds(0, 32), :]
-    for copy in near_squares:
-        copy.wait()
-    square = spart[...]
-    for i in range(peers - 1):
-        square = square + snear[i]
-    gpart[pl.ds(0, 32), :] = total
-    gpart[pl.ds(32, 8), :] = square
+        total = total + gnear[i]
+    gpart[...] = total
     gain_copies = [
         remote(gpart, gwide.at[i], g_s.at[i], g_r.at[i], there)
         for i, there in enumerate(others_of("wide"))
@@ -1196,6 +1202,10 @@
     for copy in gain_copies:
         copy.start()
     gather4[1].relay()
+    for b in range(2):
+        gather3[b].arrive()
+    layer_store = pltpu.make_async_copy(layer_ref, layer_hbm, out_sem.at[0])
+    layer_store.start()
     for copy in gain_copies:
         copy.wait()
     total = gpart[...]
@@ -1215,7 +1225,8 @@
     grad_store = pltpu.make_async_copy(grad_ref, grad_hbm, out_sem.at[1])
     grad_store.start()
     for b in range(2):
-        for each in (sums3[b], sums4[b], gather3[b], gather4[b], pair_mates[b], pair_trees[b]):
+        sums3[b].drain((5, 6) if b in EARLY else range(7))
+        for each in (sums4[b], gather3[b], gather4[b], pair_mates[b], pair_trees[b]):
             each.drain()
         grads_there[b].wait_send()
         query_back(b).wait_send()
@@ -1226,13 +1237,13 @@
 
 
 def backward(
-    lengths, gains, tables, logs, mixed, gain2, dob, squares, qs, outs, tokens, wq, wkv, hidden, dh, gout,
-    kv, n1, wd, pgate, pup,
+    lengths, gains, tables, logs, gain2, dob, squares, qs, outs, tokens, wq, wkv, hidden, dh, gout,
+    kv, n1, part, into, pgate, pup,
 ):
     count, width = n1.shape
     rows = count // 2
     share = rows // 8
-    units = wd.shape[0]
+    units = pgate.shape[2]
     lanes = wq.shape[1]
     stack = qs.shape[2]
     wide_count = 16
@@ -1258,7 +1269,7 @@
             shape((count, width), bf16),
             shape((count, width), bf16),
         ),
-        in_specs=[pl.BlockSpec(memory_space=pltpu.SMEM)] + [here] * 13 + [anywhere] * 11,
+        in_specs=[pl.BlockSpec(memory_space=pltpu.SMEM)] + [here] * 12 + [anywhere] * 12,
         out_specs=(here,) * 7 + (anywhere,) * 2,
         scratch_shapes=[
             vmem((count, width), bf16),
@@ -1274,7 +1285,6 @@
             vmem((SLOTS, wide_share, units), bf16),
             vmem(kv.shape, bf16),
             vmem((count, width), bf16),
-            vmem(wd.shape, bf16),
             vmem((2, share, width), bf16),
             *[vmem((8, *block), bf16) for block in blocks],
             *[vmem((SLOTS, *block), bf16) for block in blocks],
@@ -1301,10 +1311,8 @@
             vmem((40, wide_share), f32),
             vmem((7, 40, wide_share), f32),
             vmem((wide_count - 1, 40, wide_share), f32),
-            vmem((8, wide_share), f32),
-            vmem((7, 8, wide_share), f32),
             vmem((wide_share, 2 * HD), f32),
-            dma((12,)),
+            dma((14,)),
             dma((2,)),
             dma((2, 2, SLOTS)),
             dma((2, 2, SLOTS)),
@@ -1322,16 +1330,16 @@
             dma((2, 2)),
             dma((wide_count - 1,)),
             dma((wide_count - 1,)),
-            dma((2, 7)),
-            dma((2, 7)),
+            dma((7,)),
+            dma((7,)),
         ],
         compiler_params=pltpu.CompilerParams(
             collective_id=2, has_side_effects=True, vmem_limit_bytes=63 * MB
         ),
         name="backward",
     )(
-        lengths, gains, *tables, logs, mixed, gain2, dob, squares, qs, outs, tokens, wq, wkv, hidden, dh,
-        gout, kv, n1, wd, pgate, pup,
+        lengths, gains, *tables, logs, gain2, dob, squares, qs, outs, tokens, wq, wkv, hidden, dh,
+        gout, kv, n1, part, into, pgate, pup,
     )
 
 
@@ -1516,14 +1524,14 @@
     pair_weight = turned(keyval_weight)
     (
         logs, grad_hidden, gain_two, grad_heads, output_grad, down_sum, squares, normed_one, pairs,
-        query_stack, out_stack, hidden, mixed, gate_part, up_part,
+        query_stack, out_stack, hidden, layer_part, layer_in, gate_part, up_part,
     ) = forward(
         lengths, inputs, norm_gains, pair_weight, tables, query_weight, output_weight, gateup_weight,
         down_weight, cotangent.reshape(token_count, model_width),
     )
     query_sum, pair_sum, output_sum, gate_sum, up_sum, gains_sum, norm, layer_rows, grad_rows = backward(
-        lengths, norm_gains, tables, logs, mixed, gain_two, grad_heads, squares, query_stack, out_stack,
-        inputs, query_weight, pair_weight, hidden, grad_hidden, output_grad, pairs, normed_one, down_weight,
+        lengths, norm_gains, tables, logs, gain_two, grad_heads, squares, query_stack, out_stack,
+        inputs, query_weight, pair_weight, hidden, grad_hidden, output_grad, pairs, normed_one, layer_part, layer_in,
         gate_part, up_part,
     )
     results = update(

time: 241 us -> 237 us (0.983)
  Pallas kernels: 238 us -> 234 us
    pallas_call x1, Pallas kernels: 122 us -> 118 us  [forward(): pl.pallas_call(forward_kernel, out_shape=(shape((8, stack), f32), shape((...]
where the time goes in v2:
time: 237 us; the launch traced here: 235 us
  Pallas kernels  234 us (99%)
    pallas_call x1, Pallas kernels, forward(): pl.pallas_call(forward_kernel, out_shape=(shape((8, stack), f32), shape((...  118 us
    pallas_call x1, Pallas kernels, backward(): pl.pallas_call(backward_kernel, out_shape=(shape((wide_share, lanes), f32...  106 us
    pallas_call x1, Pallas kernels, update(): pl.pallas_call(body, out_shape=tuple(kept * 4 + [shape(layer.shape, bf16)...  9.93 us

profile of v2, /device:TPU:1, one launch (start us, length us, event | category | flops | bytes accessed | tf_op | source)
XLA Modules:
  0.0 235.1 jit_solution(13994006804469582294)
XLA Ops:
  0.7 117.8 %forward.1 = (f32[8,512]{1,0:T(8,128)}, f32[2,32,2048]{2,1,0:T(8,128)}, f32[8,2048]{1,0:T(8,128)}, bf16[512,256]{1,0:T(8,128)(2,1)}, bf16[256,2048]{1,0:T(8,128)...) custom-call(s32[2]{0:T(128)} %len_ref.3, ...), custom_call_target="tpu_custom_call" | custom-call | tf_op jit(solution)/shard_map/forward/pallas_call | solution.py:797
  118.5 106.5 %backward.1 = (f32[128,256]{1,0:T(8,128)}, f32[128,128]{1,0:T(8,128)}, f32[256,128]{1,0:T(8,128)}, f32[128,1024]{1,0:T(8,128)}, f32[128,1024]{1,0:T(8,128)}, /*i...) custom-call(s32[2]{0:T(128)} %len_ref.3, bf16[2,2048]{1,0:T(2,128)(2,1)} %refs_2_.1, ...), custom_call_target="tpu_custom_call" | custom-call | tf_op jit(solution)/shard_map/backward/pallas_call | solution.py:1259
  225.0 9.9 %update.1 = (f32[1024,128]{1,0:T(8,128)}, f32[2,128,1024]{2,1,0:T(8,128)}, f32[256,128]{1,0:T(8,128)}, f32[128,256]{1,0:T(8,128)}, f32[128,128]{1,0:T(8,128)}, /...) custom-call(f32[8,128]{1,0:T(8,128)} %get-tuple-element.94.refs_0_, ...), custom_call_target="tpu_custom_call" | custom-call | tf_op jit(solution)/shard_map/update/pallas_call | solution.py:1466

commit v3 on v2

--- a/solution.py
+++ b/solution.py
@@ -420,12 +420,17 @@
         n1[at, :] = (values * inverse_rms(values) * gains_ref[0:1, :].astype(f32)).astype(bf16)
         return carry
 
-    lax.fori_loop(0, tokens // 64, normed, 0)
     cosine, sine = rotation((tab0, tab1, tab2, tab3, tab4), wide_me, 0, rows)
-    cosine, sine = jnp.concatenate([cosine] * 2, axis=0), jnp.concatenate([sine] * 2, axis=0)
-    value = dot_nt(n1[...], wkv_ref[...])
-    lane = lax.broadcasted_iota(jnp.int32, value.shape, 1)
-    kv[wide_me] = jnp.where(lane < HD, value * cosine + swap_halves(value) * sine, value).astype(bf16)
+
+    def own_keys(b):
+        lax.fori_loop(b * rows // 64, (b + 1) * rows // 64, normed, 0)
+        mine = pl.ds(b * rows, rows)
+        value = dot_nt(n1[mine, :], wkv_ref[...])
+        lane = lax.broadcasted_iota(jnp.int32, value.shape, 1)
+        turned = value * cosine + swap_halves(value) * sine
+        kv[wide_me, mine, :] = jnp.where(lane < HD, turned, value).astype(bf16)
+
+    own_keys(0)
     met(partners)
 
     def keys_at(b):
@@ -440,6 +445,8 @@
 
     keys[0].start()
     to_mate(0, chip, 7).start()
+    own_keys(1)
+    cosine, sine = jnp.concatenate([cosine] * 2, axis=0), jnp.concatenate([sine] * 2, axis=0)
     loads[4].wait()
     for pair in range(heads // 2):
         columns = pl.ds(pair * 2 * HD, 2 * HD)

time: 237 us -> 238 us (level)
    pallas_call x1, Pallas kernels: 106 us -> 104 us  [backward(): pl.pallas_call(backward_kernel, out_shape=(shape((wide_share, lanes), f32...]
where the time goes in v3:
time: 238 us; the launch traced here: 235 us
  Pallas kernels  234 us (98%)
    pallas_call x1, Pallas kernels, forward(): pl.pallas_call(forward_kernel, out_shape=(shape((8, stack), f32), shape((...  120 us
    pallas_call x1, Pallas kernels, backward(): pl.pallas_call(backward_kernel, out_shape=(shape((wide_share, lanes), f32...  104 us
    pallas_call x1, Pallas kernels, update(): pl.pallas_call(body, out_shape=tuple(kept * 4 + [shape(layer.shape, bf16)...  9.93 us

profile of v3, /device:TPU:1, one launch (start us, length us, event | category | flops | bytes accessed | tf_op | source)
XLA Modules:
  0.0 234.6 jit_solution(12487845686466347627)
XLA Ops:
  0.7 119.8 %forward.1 = (f32[8,512]{1,0:T(8,128)}, f32[2,32,2048]{2,1,0:T(8,128)}, f32[8,2048]{1,0:T(8,128)}, bf16[512,256]{1,0:T(8,128)(2,1)}, bf16[256,2048]{1,0:T(8,128)...) custom-call(s32[2]{0:T(128)} %len_ref.3, ...), custom_call_target="tpu_custom_call" | custom-call | tf_op jit(solution)/shard_map/forward/pallas_call | solution.py:804
  120.5 104.0 %backward.1 = (f32[128,256]{1,0:T(8,128)}, f32[128,128]{1,0:T(8,128)}, f32[256,128]{1,0:T(8,128)}, f32[128,1024]{1,0:T(8,128)}, f32[128,1024]{1,0:T(8,128)}, /*i...) custom-call(s32[2]{0:T(128)} %len_ref.3, bf16[2,2048]{1,0:T(2,128)(2,1)} %refs_2_.1, ...), custom_call_target="tpu_custom_call" | custom-call | tf_op jit(solution)/shard_map/backward/pallas_call | solution.py:1266
  224.5 9.9 %update.1 = (f32[1024,128]{1,0:T(8,128)}, f32[2,128,1024]{2,1,0:T(8,128)}, f32[256,128]{1,0:T(8,128)}, f32[128,256]{1,0:T(8,128)}, f32[128,128]{1,0:T(8,128)}, /...) custom-call(f32[8,128]{1,0:T(8,128)} %get-tuple-element.94.refs_0_, ...), custom_call_target="tpu_custom_call" | custom-call | tf_op jit(solution)/shard_map/update/pallas_call | solution.py:1473
